TPU v7x, 32 devices: a whole 2x2x4 slice. The times are simulated.
32 devices in a mesh: groups: 2 (over x), clus: 16 (over z, y, core).
Axes of the slice: x: 2, y: 2, z: 4, core: 2. Of those that a mesh axis runs over, the one named last changes fastest.
Arguments:
- mesh_current: float32 [2, 131072], P(None, ('groups', 'clus')), parts along dimension 1, may hold values from -6 to 6
- branch_entry: int32 [2, 262144], P(None, ('groups', 'clus')), parts along dimension 1, may hold values from 0 to 6143, as said below
- branch_sign: int32 [2, 262144], P(None, ('groups', 'clus')), parts along dimension 1, may hold values from 0 to 1
- need_slots: int32 [512, 128], P(('groups', 'clus')), parts along dimension 0, may hold values from -1 to 4095, as said below
- resistance: float32 [262144], P(('groups', 'clus')), parts along dimension 0, may hold values from 0.3 to 3
- near_blocks: bfloat16 [2048, 4, 128, 128], P(('groups', 'clus')), parts along dimension 0, may hold values from -0.25 to 0.25
- near_source: int32 [2048, 4], P(('groups', 'clus')), parts along dimension 0, may hold values from 0 to 63
- basis_in: bfloat16 [2048, 32, 128], P(('groups', 'clus')), parts along dimension 0, may hold values from -0.5 to 0.5
- coupling: bfloat16 [2048, 16, 32, 32], P(('groups', 'clus')), parts along dimension 0, may hold values from -0.25 to 0.25
- basis_out: bfloat16 [2048, 32, 128], P(('groups', 'clus')), parts along dimension 0, may hold values from -1 to 1
- admissible: int32 [2048, 16], P(('groups', 'clus')), parts along dimension 0, may hold values from 0 to 1023, as said below
- port_mesh: int32 [128], P('groups'), parts along dimension 0, may hold values from 0 to 65535, as said below
- port_coupling: float32 [2, 64, 64], replicated, may hold values from -0.75 to 0.75
Outputs:
- mesh_voltage: float32 [2, 131072], P(None, ('groups', 'clus')), parts along dimension 1
There are 2 independent parts, one for each index of `groups`. A program takes and returns all parts, laid end to end along the dimension named above; an argument that names none is the same for every part. Nothing has to cross between parts.
Inputs may be any that keep to these rules, and one draw needn't show every extreme that they name: `need_slots`: row d * 16 + p holds distinct meshes of device p, counted from 0 within it, in its first slots and -1 in the rest. Row d * 16 + d is all -1; row d * 16 + (d + 1) % 16 has no -1. `branch_entry`: A value below 4096 is a mesh of the branch's own device d. Any other value is 4096 + p * 128 + s with p != d and slot s of row d * 16 + p of need_slots not -1. `admissible`: entry k of row t is (t + k * 64 + o) % 1024 with 1 <= o < 64; the entries of a row are distinct and never t. `port_mesh`: distinct meshes.
All inputs are finite; a program needn't handle non-finite values.
Results may differ from a plain program's by a relative error of at most 0.0021.
Values may be sent and summed in bfloat16 or wider, within the bound.
A program may use at most 320 MiB of HBM per device.

v0:
```python
import jax
import jax.numpy as jnp
from jax import lax
from jax.sharding import PartitionSpec as P


def segment_sums(values, segment_ids, total):

    def one_part(part_values):
        return jax.ops.segment_sum(part_values, segment_ids, num_segments=total)

    return jax.vmap(one_part)(values)


def per_device(
    mesh_current,
    branch_entry,
    branch_sign,
    need_slots,
    resistance,
    near_blocks,
    near_source,
    basis_in,
    coupling,
    basis_out,
    admissible,
    port_mesh,
    port_coupling,
):
    peer_count = lax.axis_size("clus")
    mesh_dev = mesh_current.shape[1]
    slot_width = need_slots.shape[1]
    tile_dev = near_blocks.shape[0]
    tile_width = near_blocks.shape[2]
    offset = lax.axis_index("clus") * mesh_dev
    position = port_mesh - offset
    owned = (position >= 0) & (position < mesh_dev)
    owner_base = (jnp.arange(peer_count, dtype=jnp.int32) * mesh_dev)[:, None]
    slot_mesh = (owner_base + jnp.maximum(need_slots, 0)).reshape(-1)
    all_currents = lax.all_gather(mesh_current, "clus", axis=1, tiled=True)
    remote = all_currents[:, slot_mesh]
    port_value = all_currents[:, port_mesh]
    lookup_table = jnp.concatenate([mesh_current, remote], axis=1)
    orient = (2 * branch_sign - 1).astype(jnp.float32)
    branch_current = jnp.sum(orient[None] * lookup_table[:, branch_entry], axis=1)
    branch_input = branch_current.astype(jnp.bfloat16).reshape(2, tile_dev, tile_width)
    far_coeff = jnp.einsum(
        "tri,cti->ctr", basis_in, branch_input, preferred_element_type=jnp.float32
    ).astype(jnp.bfloat16)
    all_coeff = lax.all_gather(far_coeff, "clus", axis=1, tiled=True)
    near_input = branch_input[:, near_source]
    near_field = jnp.einsum(
        "tkij,ctkj->cti", near_blocks, near_input, preferred_element_type=jnp.float32
    )
    picked = all_coeff[:, admissible]
    far_mixed = jnp.einsum(
        "tkrq,ctkq->ctr", coupling, picked, preferred_element_type=jnp.float32
    ).astype(jnp.bfloat16)
    far_field = jnp.einsum("tri,ctr->cti", basis_out, far_mixed, preferred_element_type=jnp.float32)
    reactive = (near_field + far_field).reshape(2, -1)
    branch_voltage = resistance[None, :] * branch_current + jnp.stack([-reactive[1], reactive[0]])
    contributions = (orient[None] * branch_voltage[:, None, :]).reshape(2, -1)
    totals = segment_sums(
        contributions, branch_entry.reshape(-1), mesh_dev + peer_count * slot_width
    )
    local_voltage = totals[:, :mesh_dev]
    slot_voltage = totals[:, mesh_dev:]
    spread = jnp.zeros((2, peer_count * mesh_dev), jnp.float32).at[:, slot_mesh].add(slot_voltage)
    arrived = lax.psum_scatter(spread, "clus", scatter_dimension=1, tiled=True)
    mesh_voltage = local_voltage + arrived
    high = lax.Precision.HIGHEST
    real_part = jnp.dot(port_coupling[0], port_value[0], precision=high) - jnp.dot(
        port_coupling[1], port_value[1], precision=high
    )
    imag_part = jnp.dot(port_coupling[0], port_value[1], precision=high) + jnp.dot(
        port_coupling[1], port_value[0], precision=high
    )
    target_rows = jnp.where(owned, position, mesh_dev)
    mesh_voltage = mesh_voltage.at[:, target_rows].add(
        jnp.stack([real_part, imag_part]), mode="drop"
    )
    return mesh_voltage


def solution(mesh):
    in_specs = (
        P(None, ("groups", "clus")),
        P(None, ("groups", "clus")),
        P(None, ("groups", "clus")),
        P(("groups", "clus"), None),
        P(("groups", "clus")),
        P(("groups", "clus"), None, None, None),
        P(("groups", "clus"), None),
        P(("groups", "clus"), None, None),
        P(("groups", "clus"), None, None, None),
        P(("groups", "clus"), None, None),
        P(("groups", "clus"), None),
        P("groups"),
        P(),
    )
    out_specs = P(None, ("groups", "clus"))
    return jax.shard_map(
        per_device, mesh=mesh, in_specs=in_specs, out_specs=out_specs, check_vma=False
    )
```

profile of v0, /device:TPU:0, one launch (start us, length us, event | category | flops | bytes accessed | tf_op | source)
XLA Modules:
  0.0 998.0 jit_solution(3522552970147552140)
XLA Ops:
  6.5 0.7 compare_select_fusion.3
  7.3 0.8 maximum_add_fusion
  8.1 0.7 compare_select_fusion.2
  9.2 0.9 fusion.15
  10.1 0.8 copy.62
  10.9 0.9 fusion.29
  11.8 1.4 copy.50
  13.2 13.3 %copy.55 = bf16[64,16,32,32]{3,2,1,0:T(8,128)(2,1)} copy(bf16[64,16,32,32]{0,3,2,1:T(8,128)(2,1)} %param.21) | data formatting | bytes 4194304 | tf_op args[8]
  26.6 331.8 %all_gather.6 = f32[2,65536]{0,1:T(8,128)} all-gather(f32[2,4096]{0,1:T(8,128)S(1)} %copy.50), channel_id=1, replica_groups=mesh['groups'=2,'clus'=16] {'clus'}, dimensions={1}, use_global_device_ids=true | all-gather | bytes 557056 | tf_op jit(solution)/shard_map/all_gather | solution.py:40
  358.4 18.1 %gather_fusion = f32[2048,2]{1,0:T(8,128)} fusion(f32[2,65536]{0,1:T(8,128)} %all_gather.6, s32[2048]{0:T(1024)S(1)} %broadcast_clamp_fusion.1), kind=kCustom, calls=%fused_computation | custom fusion | bytes 40960 | tf_op jit(solution)/shard_map/gather | solution.py:41
  376.5 3.0 pad_maximum_fusion
  379.5 56.3 %gather_fusion.1 = f32[16384,2]{1,0:T(8,128)} fusion(f32[2,6144]{0,1:T(8,128)} %pad_maximum_fusion, s32[16384]{0:T(1024)S(1)} %broadcast_clamp_fusion), kind=kCustom, calls=%fused_computation.1 | custom fusion | bytes 327680 | tf_op jit(solution)/shard_map/gather | solution.py:45
  435.8 5.5 multiply_reduce_fusion
  441.5 1.2 copy-done.3
  442.7 0.7 fusion.10
  443.4 63.3 %all_gather.7 = bf16[2,1024,32]{2,0,1:T(2,128)(2,1)S(1)} all-gather(bf16[2,64,32]{2,0,1:T(2,128)(2,1)S(1)} %fusion.10), channel_id=1, replica_groups=mesh['groups'=2,'clus'=16] {'clus'}, dimensions={1}, use_global_device_ids=true | all-gather | bytes 139264 | tf_op jit(solution)/shard_map/all_gather | solution.py:50
  506.7 8.6 gather_fusion.2
  515.3 6.4 copy.52
  521.7 3.7 gather_fusion.3
  525.4 5.8 fusion.9
  531.1 5.7 fusion.6
  537.0 2.7 copy.56
  539.7 4.1 bitcast_add_fusion
  543.8 4.6 bitcast_multiply_fusion
  548.4 81.5 %scatter_custom_fusion = f32[2,6144]{0,1:T(8,128)} fusion(s32[16384]{0:T(1024)S(1)} %bitcast.119, f32[2,16384]{0,1:T(8,128)} %bitcast_multiply_fusion, f32[]{:T(128)} %constant.10.clone.1), kind=kCustom, calls=%fused_computation.10 | custom fusion | flops 32768 | bytes 180228 | tf_op jit(solution)/shard_map/vmap()/scatter-add | solution.py:10
  630.0 26.1 %scatter_custom_fusion.1 = f32[2,65536]{0,1:T(8,128)} fusion(s32[2048]{0:T(1024)S(1)} %bitcast.121, f32[]{:T(128)} %constant.10.clone.1, f32[2,6144]{0,1:T(8,128)} %scatter_custom_fusion), kind=kCustom, calls=%fused_computation.8 | custom fusion | flops 4096 | bytes 1573376 | tf_op jit(solution)/shard_map/scatter-add | solution.py:68
  656.1 0.6 copy-done.6
  656.8 16.4 %gather_fusion.4 = f32[64,2]{1,0:T(8,128)S(1)} fusion(f32[2,65536]{0,1:T(8,128)} %all_gather.6, s32[1024]{0:T(1024)S(1)} %pad_clamp_fusion), kind=kCustom, calls=%fused_computation.4 | custom fusion | bytes 1280 | tf_op jit(solution)/shard_map/gather | solution.py:42
  674.1 311.7 %reduce-scatter.2.cloned.1.call-done = f32[2,4096]{0,1:T(8,128)} async-done(((f32[2,65536]{0,1:T(8,128)}), f32[2,4096]{0,1:T(8,128)}) %reduce-scatter.2.cloned.1.call-update) | async-done | bytes 32784 | tf_op jit(solution)/shard_map/reduce_scatter | solution.py:69
  985.8 2.4 slice_add_fusion
  988.3 1.7 scatter_fusion
  990.0 1.2 copy.58
  (38 shorter events, 1.8 us)
Async XLA Ops:
  6.5 518.8 %copy-start = (bf16[64,32,128]{2,1,0:T(8,128)(2,1)S(1)}, bf16[64,32,128]{2,1,0:T(8,128)(2,1)}, u32[]{:S(2)}) copy-start(bf16[64,32,128]{2,1,0:T(8,128)(2,1)} %param.22) | copy-start | bytes 1572868
  6.5 979.3 %reduce-scatter.2.cloned.1.call-start = ((), (), s32[]{:S(2)}) async-start(), calls=%async_computation.1 | async-start | bytes 35651584 | tf_op jit(solution)/shard_map/reduce_scatter | solution.py:69
  441.3 2.1 copy-start.2
  441.3 1.4 copy-start.3
  536.8 2.9 copy-start.5
  656.1 0.7 copy-start.6
  656.1 17.2 %copy-start.4 = (f32[2,64,64]{2,1,0:T(8,128)S(1)}, f32[2,64,64]{2,1,0:T(8,128)}, u32[]{:S(2)}) copy-start(f32[2,64,64]{2,1,0:T(8,128)} %param.25) | copy-start | bytes 98308
  674.0 317.2 %copy-start.1 = (bf16[64,32,128]{2,1,0:T(8,128)(2,1)S(1)}, bf16[64,32,128]{2,1,0:T(8,128)(2,1)}, u32[]{:S(2)}) copy-start(bf16[64,32,128]{2,1,0:T(8,128)(2,1)} %param.22) | copy-start | bytes 1572868
Sparse Core Ops, SparseCore 0:
  656.2 329.5 reduce-scatter.1
where the time goes:
time: 999 us; the launch traced here: 998 us
  blocking collectives  395 us (40%)
  waiting for transfers between devices  312 us (31%)
  other arithmetic  133 us (13%)
  local copies, waits for them, and re-layouts  131 us (13%)
  between operations  13.6 us (1%)
  matrix products  12.8 us (1%)
    all_gather x1, blocking collectives, per_device(): all_currents = lax.all_gather(mesh_current, 'clus', axis=1, tiled=True)  332 us
    reduce_scatter x1, waiting for transfers between devices, per_device(): arrived = lax.psum_scatter(spread, 'clus', scatter_dimension=1, tiled=True)  312 us
    scatter-add x1, other arithmetic, one_part(): return jax.ops.segment_sum(part_values, segment_ids, num_segments=total)  81.5 us
    all_gather x1, blocking collectives, per_device(): all_coeff = lax.all_gather(far_coeff, 'clus', axis=1, tiled=True)  63.3 us
    gather x1, local copies, waits for them, and re-layouts, per_device(): lookup_table[:, branch_entry]  56.3 us
    scatter-add x1, other arithmetic, per_device(): jnp.zeros((2, peer_count * mesh_dev), jnp.float32).at[:, slot_mesh]  26.1 us
  transfers between devices with their start and end apart: 1, of which 1 were waited for; matrix products, arithmetic and copies ran while one was open for 2% of the time, Pallas kernels for 0%

commit v1 on v0

v1 whole, which is shorter than its diff:
```python
import functools

import jax
import jax.numpy as jnp
from jax import lax
from jax.experimental import pallas as pl
from jax.experimental.pallas import tpu as pltpu
from jax.sharding import PartitionSpec as P

LANES = 128
CHUNK = 1024
VMEM_LIMIT = 48 * 1024 * 1024
NT = (((1,), (1,)), ((), ()))


def exchange_kernel(peers, gather, x_ref, o_ref, send_sem, recv_sem, own_sem):
    me = lax.axis_index("clus")

    def peer_at(step):
        return lax.rem(me + step, peers)

    def copy_at(step):
        peer = peer_at(step)
        return pltpu.make_async_remote_copy(
            src_ref=x_ref if gather else x_ref.at[peer],
            dst_ref=o_ref.at[me],
            send_sem=send_sem.at[step],
            recv_sem=recv_sem.at[step],
            device_id={"clus": peer},
            device_id_type=pl.DeviceIdType.MESH,
        )

    barrier = pltpu.get_barrier_semaphore()

    @pl.loop(1, peers)
    def _(step):
        pl.semaphore_signal(
            barrier, inc=1, device_id={"clus": peer_at(step)}, device_id_type=pl.DeviceIdType.MESH
        )

    own = pltpu.make_async_copy(x_ref if gather else x_ref.at[me], o_ref.at[me], own_sem)
    own.start()
    pl.semaphore_wait(barrier, peers - 1)

    @pl.loop(1, peers)
    def _(step):
        copy_at(step).start()

    own.wait()

    @pl.loop(1, peers)
    def _(step):
        copy_at(step).wait()


def exchange(x, peers, collective_id, gather=False):
    shape = (peers,) + (x.shape if gather else x.shape[1:])
    return pl.pallas_call(
        functools.partial(exchange_kernel, peers, gather),
        out_shape=jax.ShapeDtypeStruct(shape, x.dtype),
        in_specs=[pl.BlockSpec(memory_space=pltpu.VMEM)],
        out_specs=pl.BlockSpec(memory_space=pltpu.VMEM),
        scratch_shapes=[
            pltpu.SemaphoreType.DMA((peers,)),
            pltpu.SemaphoreType.DMA((peers,)),
            pltpu.SemaphoreType.DMA,
        ],
        compiler_params=pltpu.CompilerParams(collective_id=collective_id, has_side_effects=True),
    )(x)


def split(value):
    high = value.astype(jnp.bfloat16).astype(jnp.float32)
    return high, value - high


def lanes_one_hot(index):
    low = index & (LANES - 1)
    rows = lax.broadcasted_iota(jnp.int32, (LANES, index.shape[1]), 0)
    return jnp.where(rows == low, 1.0, 0.0).astype(jnp.bfloat16)


def rows_mask(index, rows):
    return lax.broadcasted_iota(jnp.int32, (rows, index.shape[1]), 0) == (index >> 7)


def lookup_operand(tables):
    high, low = split(jnp.concatenate(tables, axis=0))
    return jnp.concatenate([high.astype(jnp.bfloat16), low.astype(jnp.bfloat16)], axis=1)


def look_up(operand, index, rows):
    hot = lanes_one_hot(index)
    found = jnp.dot(
        operand, jnp.concatenate([hot, hot], axis=0), preferred_element_type=jnp.float32
    )
    mask = rows_mask(index, rows)
    return [
        jnp.sum(jnp.where(mask, found[c * rows : (c + 1) * rows], 0.0), axis=0, keepdims=True)
        for c in range(2)
    ]


def sums(values, index, rows):
    hot = lanes_one_hot(index)
    mask = rows_mask(index, rows)
    parts = [split(value) for value in values]
    spread = [
        jnp.where(mask, parts[c][part], 0.0).astype(jnp.bfloat16)
        for part in range(2)
        for c in range(2)
    ]
    made = lax.dot_general(
        jnp.concatenate(spread, axis=0), hot, NT, preferred_element_type=jnp.float32
    )
    return made[: 2 * rows] + made[2 * rows :]


def row_of(ref, row, peers):
    return jnp.concatenate([ref[p, row : row + 1, :] for p in range(peers)], axis=1)


def answer_kernel(peers, mesh_rows, current_ref, asked_ref, port_ref, o_ref):
    operand = lookup_operand([current_ref[0], current_ref[1]])
    o_ref[...] = jnp.zeros_like(o_ref)
    asked = look_up(operand, row_of(asked_ref, 0, peers), mesh_rows)
    ports = look_up(operand, port_ref[...], mesh_rows)
    for p in range(peers):
        for c in range(2):
            o_ref[p, c : c + 1, :] = asked[c][:, p * LANES : (p + 1) * LANES]
            o_ref[p, 2 + c : 3 + c, :] = ports[c]


def branch_kernel(
    peers, rows, current_ref, remote_ref, entry_ref, sign_ref, basis_ref, flow_ref, coeff_ref
):
    operand = lookup_operand(
        [
            part
            for c in range(2)
            for part in [current_ref[c]] + [remote_ref[p, c : c + 1, :] for p in range(peers)]
        ]
    )

    @pl.loop(0, entry_ref.shape[1] // CHUNK)
    def _(step):
        columns = pl.ds(pl.multiple_of(step * CHUNK, CHUNK), CHUNK)
        total = [0.0, 0.0]
        for k in range(entry_ref.shape[0]):
            orient = (2 * sign_ref[k : k + 1, columns] - 1).astype(jnp.float32)
            found = look_up(operand, entry_ref[k : k + 1, columns], rows)
            total = [total[c] + orient * found[c] for c in range(2)]
        tiles = CHUNK // LANES
        for c in range(2):
            flow_ref[c, pl.ds(pl.multiple_of(step * tiles, tiles), tiles), :] = jnp.concatenate(
                [total[c][:, j * LANES : (j + 1) * LANES] for j in range(tiles)], axis=0
            )

    tile_dev = flow_ref.shape[1]
    rank = basis_ref.shape[0] // tile_dev
    width = 512
    for start in range(0, basis_ref.shape[0], width):
        basis = basis_ref[start : start + width, :]
        own = lax.broadcasted_iota(jnp.int32, (tile_dev, width), 0) == (
            lax.broadcasted_iota(jnp.int32, (tile_dev, width), 1) + start
        ) // rank
        for c in range(2):
            crossed = lax.dot_general(
                flow_ref[c].astype(jnp.bfloat16), basis, NT, preferred_element_type=jnp.float32
            )
            coeff_ref[c : c + 1, start : start + width] = jnp.sum(
                jnp.where(own, crossed, 0.0), axis=0, keepdims=True
            )


def collect_kernel(rows, voltage_ref, entry_ref, sign_ref, o_ref):
    o_ref[...] = jnp.zeros_like(o_ref)

    @pl.loop(0, entry_ref.shape[1] // CHUNK)
    def _(step):
        columns = pl.ds(pl.multiple_of(step * CHUNK, CHUNK), CHUNK)
        for k in range(entry_ref.shape[0]):
            orient = (2 * sign_ref[k : k + 1, columns] - 1).astype(jnp.float32)
            values = [orient * voltage_ref[c : c + 1, columns] for c in range(2)]
            o_ref[...] += sums(values, entry_ref[k : k + 1, columns], rows)


def finish_kernel(
    peers, rows, mesh_rows, sums_ref, arrived_ref, asked_ref, answer_ref, port_ref, z_ref, o_ref
):
    asked = row_of(asked_ref, 0, peers)
    arrived = sums([row_of(arrived_ref, c, peers) for c in range(2)], asked, mesh_rows)
    current = answer_ref[0]
    for p in range(1, peers):
        current = current + answer_ref[p]
    products = [
        lax.dot_general(
            current,
            z_ref[part],
            NT,
            precision=lax.Precision.HIGHEST,
            preferred_element_type=jnp.float32,
        )
        for part in range(2)
    ]
    real_part = products[0][2:3] - products[1][3:4]
    imag_part = products[0][3:4] + products[1][2:3]
    ports = sums([real_part, imag_part], port_ref[...], mesh_rows)
    for c in range(2):
        own = slice(c * mesh_rows, (c + 1) * mesh_rows)
        o_ref[c] = sums_ref[c * rows : c * rows + mesh_rows, :] + arrived[own] + ports[own]


def local_call(body, shapes, *arrays):
    return pl.pallas_call(
        body,
        out_shape=shapes,
        compiler_params=pltpu.CompilerParams(vmem_limit_bytes=VMEM_LIMIT),
    )(*arrays)


def f32(*shape):
    return jax.ShapeDtypeStruct(shape, jnp.float32)


def per_device(
    mesh_current,
    branch_entry,
    branch_sign,
    need_slots,
    resistance,
    near_blocks,
    near_source,
    basis_in,
    coupling,
    basis_out,
    admissible,
    port_mesh,
    port_coupling,
):
    peers = lax.axis_size("clus")
    mesh_dev = mesh_current.shape[1]
    branch_dev = branch_entry.shape[1]
    tile_dev, near_count, tile_width = near_blocks.shape[:3]
    rank = basis_in.shape[1]
    ports = port_mesh.shape[0]
    mesh_rows = mesh_dev // LANES
    rows = mesh_rows + peers
    current = mesh_current.reshape(2, mesh_rows, LANES)
    offset = lax.axis_index("clus") * mesh_dev
    port_position = jnp.pad(port_mesh, (0, LANES - ports), constant_values=-1)[None, :] - offset
    impedance = jnp.pad(port_coupling, ((0, 0), (0, LANES - ports), (0, LANES - ports)))

    asked = exchange(jnp.pad(need_slots[:, None, :], ((0, 0), (0, 7), (0, 0))), peers, 0)
    answer = exchange(
        local_call(
            functools.partial(answer_kernel, peers, mesh_rows),
            f32(peers, 8, LANES),
            current,
            asked,
            port_position,
        ),
        peers,
        1,
    )
    flow, coeff = local_call(
        functools.partial(branch_kernel, peers, rows),
        [f32(2, tile_dev, LANES), f32(2, tile_dev * rank)],
        current,
        answer,
        branch_entry,
        branch_sign,
        basis_in.reshape(tile_dev * rank, tile_width),
    )
    branch_input = flow.astype(jnp.bfloat16)
    mine = coeff.astype(jnp.bfloat16).reshape(-1, LANES)
    all_coeff = exchange(mine, peers, 2, gather=True)

    near_hot = jax.nn.one_hot(near_source.reshape(-1), tile_dev, dtype=jnp.bfloat16)
    near_input = jnp.einsum(
        "ns,csj->cnj", near_hot, branch_input, preferred_element_type=jnp.bfloat16
    ).reshape(2, tile_dev, near_count, tile_width)
    near_field = jnp.einsum(
        "tkij,ctkj->cti", near_blocks, near_input, preferred_element_type=jnp.float32
    )
    table = all_coeff.reshape(peers, 2, tile_dev, rank).transpose(0, 2, 1, 3)
    far_hot = jax.nn.one_hot(admissible.reshape(-1), peers * tile_dev, dtype=jnp.bfloat16)
    picked = jnp.dot(
        far_hot,
        table.reshape(peers * tile_dev, 2 * rank),
        preferred_element_type=jnp.bfloat16,
    ).reshape(tile_dev, -1, 2, rank)
    far_mixed = jnp.einsum(
        "tkrq,tkcq->ctr", coupling, picked, preferred_element_type=jnp.float32
    ).astype(jnp.bfloat16)
    far_field = jnp.einsum("tri,ctr->cti", basis_out, far_mixed, preferred_element_type=jnp.float32)
    reactive = near_field + far_field
    resistive = resistance.reshape(1, tile_dev, tile_width) * flow
    voltage = (resistive + jnp.stack([-reactive[1], reactive[0]])).reshape(2, branch_dev)

    totals = local_call(
        functools.partial(collect_kernel, rows),
        f32(2 * rows, LANES),
        voltage,
        branch_entry,
        branch_sign,
    )
    slots = totals.reshape(2, rows, LANES)[:, mesh_rows:].transpose(1, 0, 2)
    arrived = exchange(jnp.pad(slots, ((0, 0), (0, 6), (0, 0))), peers, 3)
    made = local_call(
        functools.partial(finish_kernel, peers, rows, mesh_rows),
        f32(2, mesh_rows, LANES),
        totals,
        arrived,
        asked,
        answer,
        port_position,
        impedance,
    )
    return made.reshape(2, mesh_dev)


def solution(mesh):
    in_specs = (
        P(None, ("groups", "clus")),
        P(None, ("groups", "clus")),
        P(None, ("groups", "clus")),
        P(("groups", "clus"), None),
        P(("groups", "clus")),
        P(("groups", "clus"), None, None, None),
        P(("groups", "clus"), None),
        P(("groups", "clus"), None, None),
        P(("groups", "clus"), None, None, None),
        P(("groups", "clus"), None, None),
        P(("groups", "clus"), None),
        P("groups"),
        P(),
    )
    out_specs = P(None, ("groups", "clus"))
    return jax.shard_map(
        per_device, mesh=mesh, in_specs=in_specs, out_specs=out_specs, check_vma=False
    )
```

time: 999 us -> 86.2 us (0.09)
  blocking collectives: 395 us -> 0 us
  waiting for transfers between devices: 312 us -> 0 us
  other arithmetic: 133 us -> 0.71 us
  local copies, waits for them, and re-layouts: 131 us -> 28.4 us
  Pallas kernels: 0 us -> 44 us
  between operations: 13.6 us -> 0.29 us
    all_gather x2 -> x0, blocking collectives: 395 us -> none  [the longest x1 332 us: per_device(): all_currents = lax.all_gather(mesh_current, 'clus', axis=1, tiled=True)]
    reduce_scatter x1 -> x0, waiting for transfers between devices: 312 us -> none  [per_device(): arrived = lax.psum_scatter(spread, 'clus', scatter_dimension=1, tiled=True)]
    gather x6 -> x0, local copies, waits for them, and re-layouts: 109 us -> none  [the longest x1 56.3 us: per_device(): lookup_table[:, branch_entry]]
    scatter-add x3 -> x0, other arithmetic: 109 us -> none  [the longest x1 81.5 us: one_part(): return jax.ops.segment_sum(part_values, segment_ids, num_segments=total)]
    pallas_call x0 -> x8, Pallas kernels: none -> 44 us  [the longest x4 36.6 us: exchange(): pl.pallas_call(functools.partial(exchange_kernel, peers, gather), out_sha...]
    unnamed x19 -> x37, local copies, waits for them, and re-layouts: 17.4 us -> 23.9 us
  transfers between devices with their start and end apart: 1 -> 0, of which waited for: 1 -> 0; matrix products, arithmetic and copies ran while one was open for 2% -> 0% of each run, Pallas kernels for 0% -> 0%
where the time goes in v1:
time: 86.2 us; the launch traced here: 85.4 us
  Pallas kernels  44 us (51%)
  local copies, waits for them, and re-layouts  28.4 us (33%)
  matrix products  12 us (14%)
    pallas_call x4, Pallas kernels, exchange(): pl.pallas_call(functools.partial(exchange_kernel, peers, gather), out_sha...  36.6 us
    unnamed x37, local copies, waits for them, and re-layouts  23.9 us
    pallas_call x4, Pallas kernels, local_call(): pl.pallas_call(body, out_shape=shapes, compiler_params=pltpu.CompilerPara...  7.39 us
    dot_general x1, matrix products, per_device(): jnp.einsum('tkij,ctkj->cti', near_blocks, near_input, preferred_element_t...  5.68 us
    dot_general x1, matrix products, per_device(): jnp.einsum('tri,ctr->cti', basis_out, far_mixed, preferred_element_type=j...  5.23 us

profile of v1, /device:TPU:0, one launch (start us, length us, event | category | flops | bytes accessed | tf_op | source)
XLA Modules:
  0.0 85.4 jit_solution(5274061762744967540)
XLA Ops:
  0.0 1.4 %pad.16.x_ref = s32[16,8,128]{2,1,0:T(8,128)} pad(s32[16,1,128]{2,1,0:T(1,128)} %bitcast.78, s32[]{:T(128)} %constant.2.clone.1), padding=0_0x0_7x0_0 | pad | bytes 73732 | tf_op jit(solution)/shard_map/jit(_pad)/pad | solution.py:254
  1.4 10.3 %shard_map.127.asked_ref = s32[16,8,128]{2,1,0:T(8,128)} custom-call(s32[16,8,128]{2,1,0:T(8,128)} %pad.16.x_ref), custom_call_target="tpu_custom_call" | custom-call | tf_op jit(solution)/shard_map/pallas_call | solution.py:58
  11.7 0.8 copy.50
  12.5 0.7 subtract_bitcast_fusion.port_ref
  13.2 0.8 copy-done.3
  14.0 0.4 shard_map.128.x_ref
  14.4 0.6 copy-done.11
  15.0 8.3 %shard_map.129.remote_ref.answer_ref = f32[16,8,128]{2,1,0:T(8,128)} custom-call(f32[16,8,128]{2,1,0:T(8,128)} %copy-done.11), custom_call_target="tpu_custom_call" | custom-call | tf_op jit(solution)/shard_map/pallas_call | solution.py:58
  23.3 0.8 copy-done.1
  24.2 1.0 %copy-done.5 = bf16[64,32,128]{2,1,0:T(8,128)(2,1)S(1)} copy-done((bf16[64,32,128]{2,1,0:T(8,128)(2,1)S(1)}, bf16[64,32,128]{2,1,0:T(8,128)(2,1)}, u32[]{:S(2)}) %copy-start.5) | copy-done | bytes 524312
  25.2 0.8 copy-done.7
  26.0 0.8 copy-done.9
  26.9 3.4 %shard_map.130 = (f32[2,64,128]{2,1,0:T(8,128)S(1)}, f32[2,2048]{1,0:T(2,128)S(1)}) custom-call(f32[2,32,128]{2,1,0:T(8,128)S(1)} %bitcast.68, f32[16,8,128]{2,1,0:T(8,128)S(1)} %copy-done.1, s32[2,8192]{1,0:T(2,128)S(1)} %copy-done.7, s32[2,8192]{1,0:T(2,128)S(1)} %copy-done.9, bf16[2048,128]{1,0:T(8,128)(2,1)S(1)} %bitcast.66), custom_call_target="tpu_custom_call" | custom-call | tf_op jit(solution)/shard_map/pallas_call | solution.py:215
  30.3 0.8 copy.18
  31.1 0.1 eq.58
  31.2 0.2 convolution_bitcast_fusion
  31.4 0.1 copy.19
  31.5 5.7 %convolution_bitcast_fusion.2 = f32[64,2,128]{2,1,0:T(2,128)S(1)} fusion(bf16[64,4,128,128]{3,2,1,0:T(8,128)(2,1)} %param.18, bf16[2,64,4,128]{3,2,1,0:T(4,128)(2,1)S(1)} %bitcast.73), kind=kOutput, calls=%fused_computation.6 | convolution fusion | flops 16777216 | bytes 8585216 | tf_op jit(solution)/shard_map/tkij,ctkj->cti/dot_general | solution.py:283
  37.2 0.6 reshape.62.x_ref
  37.8 9.3 %shard_map.131 = bf16[16,32,128]{2,1,0:T(8,128)(2,1)} custom-call(bf16[32,128]{1,0:T(8,128)(2,1)} %reshape.62.x_ref), custom_call_target="tpu_custom_call" | custom-call | tf_op jit(solution)/shard_map/pallas_call | solution.py:58
  47.1 1.1 %reshape.63 = bf16[16,2,64,32]{3,2,1,0:T(8,128)(2,1)S(1)} reshape(bf16[16,32,128]{2,1,0:T(8,128)(2,1)} %shard_map.131) | data formatting | bytes 262144 | tf_op jit(solution)/shard_map/reshape | solution.py:286
  48.2 0.3 copy.22
  48.5 0.2 reshape.64
  48.8 0.9 %fusion.1 = bf16[64,16,2,32]{3,1,2,0:T(8,128)(2,1)S(1)} fusion(bf16[2,32,1024,1]{2,1,0,3:T(8,128)(2,1)S(1)} %bitcast.74, s32[64,16]{1,0:T(8,128)S(1)} %copy.21), kind=kOutput, calls=%fused_computation.2 | convolution fusion | flops 135266304 | bytes 266240 | tf_op jit(solution)/shard_map/dot_general | solution.py:288
  49.7 15.7 %copy.29 = bf16[64,16,32,32]{2,3,1,0:T(8,128)(2,1)} copy(bf16[64,16,32,32]{0,3,2,1:T(8,128)(2,1)} %param.21) | data formatting | bytes 4194304 | tf_op args[8]
  65.5 5.2 %fusion.6 = f32[64,2,128]{2,1,0:T(2,128)S(1)} fusion(bf16[64,32,128]{2,1,0:T(8,128)(2,1)S(1)} %copy-done, bf16[64,16,32,32]{2,3,1,0:T(8,128)(2,1)} %copy.29, bf16[64,16,2,32]{3,1,2,0:T(8,128)(2,1)S(1)} %fusion.1), kind=kOutput, calls=%fused_computation.9 | convolution fusion | flops 5246976 | bytes 2818048 | tf_op jit(solution)/shard_map/tri,ctr->cti/dot_general | solution.py:296
  70.8 3.0 %shard_map.132.sums_ref = f32[96,128]{1,0:T(8,128)S(1)} custom-call(f32[2,8192]{1,0:T(2,128)S(1)} %bitcast.70, s32[2,8192]{1,0:T(2,128)S(1)} %copy-done.8, s32[2,8192]{1,0:T(2,128)S(1)} %copy-done.10), custom_call_target="tpu_custom_call" | custom-call | tf_op jit(solution)/shard_map/pallas_call | solution.py:215
  73.9 0.6 pad.18.x_ref
  74.5 8.7 %shard_map.133.arrived_ref = f32[16,8,128]{2,1,0:T(8,128)} custom-call(f32[16,8,128]{2,1,0:T(8,128)} %pad.18.x_ref), custom_call_target="tpu_custom_call" | custom-call | tf_op jit(solution)/shard_map/pallas_call | solution.py:58
  83.3 0.8 copy-done.6
  84.1 0.6 shard_map.134
  84.7 0.7 copy.49
  (32 shorter events, 0.3 us)
Async XLA Ops:
  0.0 65.4 %copy-start = (bf16[64,32,128]{2,1,0:T(8,128)(2,1)S(1)}, bf16[64,32,128]{2,1,0:T(8,128)(2,1)}, u32[]{:S(2)}) copy-start(bf16[64,32,128]{2,1,0:T(8,128)(2,1)} %param.22) | copy-start | bytes 1572868
  0.0 48.7 %copy-start.14 = (s32[64,16]{0,1:T(8,128)S(1)}, s32[64,16]{0,1:T(8,128)}, u32[]{:S(2)}) copy-start(s32[64,16]{0,1:T(8,128)} %param.23) | copy-start | bytes 12292
  13.2 0.8 copy-start.3
  14.4 0.6 copy-start.11
  23.3 0.8 copy-start.1
  24.2 1.0 %copy-start.5 = (bf16[64,32,128]{2,1,0:T(8,128)(2,1)S(1)}, bf16[64,32,128]{2,1,0:T(8,128)(2,1)}, u32[]{:S(2)}) copy-start(bf16[64,32,128]{2,1,0:T(8,128)(2,1)} %param.20) | copy-start | bytes 1572868
  25.2 0.8 copy-start.7
  26.0 0.8 copy-start.9
  65.4 5.3 %copy-start.13 = (f32[8192]{0:T(1024)S(1)}, f32[8192]{0:T(1024)}, u32[]{:S(2)}) copy-start(f32[8192]{0:T(1024)} %param.17) | copy-start | bytes 98308
  65.4 5.4 %copy-start.8 = (s32[2,8192]{1,0:T(2,128)S(1)}, s32[2,8192]{1,0:T(2,128)}, u32[]{:S(2)}) copy-start(s32[2,8192]{1,0:T(2,128)} %entry_ref.3) | copy-start | bytes 196612
  65.4 5.4 %copy-start.10 = (s32[2,8192]{1,0:T(2,128)S(1)}, s32[2,8192]{1,0:T(2,128)}, u32[]{:S(2)}) copy-start(s32[2,8192]{1,0:T(2,128)} %sign_ref.3) | copy-start | bytes 196612
  65.4 17.8 %copy-start.12 = (f32[2,64,64]{2,1,0:T(8,128)S(1)}, f32[2,64,64]{2,1,0:T(8,128)}, u32[]{:S(2)}) copy-start(f32[2,64,64]{2,1,0:T(8,128)} %param.25) | copy-start | bytes 98308
  65.4 17.8 %copy-start.2 = (f32[16,8,128]{2,1,0:T(8,128)S(1)}, f32[16,8,128]{2,1,0:T(8,128)}, u32[]{:S(2)}) copy-start(f32[16,8,128]{2,1,0:T(8,128)} %shard_map.129.remote_ref.answer_ref) | copy-start | bytes 196612
  65.4 17.8 %copy-start.4 = (s32[16,8,128]{2,1,0:T(8,128)S(1)}, s32[16,8,128]{2,1,0:T(8,128)}, u32[]{:S(2)}) copy-start(s32[16,8,128]{2,1,0:T(8,128)} %shard_map.127.asked_ref) | copy-start | bytes 196612
  83.3 0.8 copy-start.6

commit v2 on v1

--- a/solution.py
+++ b/solution.py
@@ -13,7 +13,10 @@
 NT = (((1,), (1,)), ((), ()))
 
 
-def exchange_kernel(peers, gather, x_ref, o_ref, send_sem, recv_sem, own_sem):
+def exchange_kernel(peers, gather, work, x_ref, *refs):
+    *work_ins, o_ref, send_sem, recv_sem, own_sem = refs
+    if work is not None:
+        *work_ins, o_ref, work_out, send_sem, recv_sem, own_sem, work_scratch = refs
     me = lax.axis_index("clus")
 
     def peer_at(step):
@@ -47,26 +50,66 @@
         copy_at(step).start()
 
     own.wait()
+    if work is not None:
+        work(*work_ins, work_out, work_scratch)
 
     @pl.loop(1, peers)
     def _(step):
         copy_at(step).wait()
 
 
-def exchange(x, peers, collective_id, gather=False):
+def exchange(x, peers, collective_id, gather=False, work=None, extra=(), made=(), scratch=()):
     shape = (peers,) + (x.shape if gather else x.shape[1:])
-    return pl.pallas_call(
-        functools.partial(exchange_kernel, peers, gather),
-        out_shape=jax.ShapeDtypeStruct(shape, x.dtype),
-        in_specs=[pl.BlockSpec(memory_space=pltpu.VMEM)],
-        out_specs=pl.BlockSpec(memory_space=pltpu.VMEM),
+    vmem = pl.BlockSpec(memory_space=pltpu.VMEM)
+    out = pl.pallas_call(
+        functools.partial(exchange_kernel, peers, gather, work),
+        out_shape=[jax.ShapeDtypeStruct(shape, x.dtype), *made],
+        in_specs=[vmem] * (1 + len(extra)),
+        out_specs=[vmem] * (1 + len(made)),
         scratch_shapes=[
             pltpu.SemaphoreType.DMA((peers,)),
             pltpu.SemaphoreType.DMA((peers,)),
             pltpu.SemaphoreType.DMA,
+            *scratch,
         ],
-        compiler_params=pltpu.CompilerParams(collective_id=collective_id, has_side_effects=True),
-    )(x)
+        compiler_params=pltpu.CompilerParams(
+            collective_id=collective_id, has_side_effects=True, vmem_limit_bytes=VMEM_LIMIT
+        ),
+    )(x, *extra)
+    return out if made else out[0]
+
+
+def near_work(flow_ref, source_ref, blocks_ref, near_ref, picked_ref):
+    tile_dev, near_count = blocks_ref.shape[:2]
+    count = source_ref.shape[0]
+    hot = jnp.where(
+        lax.broadcasted_iota(jnp.int32, (count, tile_dev), 1) == source_ref[...], 1.0, 0.0
+    ).astype(jnp.bfloat16)
+    for c in range(2):
+        picked_ref[c] = jnp.dot(
+            hot, flow_ref[c].astype(jnp.bfloat16), preferred_element_type=jnp.float32
+        )
+
+    @pl.loop(0, tile_dev // 8)
+    def _(step):
+        rows = []
+        for j in range(8):
+            tile = step * 8 + j
+            total = 0.0
+            for k in range(near_count):
+                place = pl.ds(tile * near_count + k, 1)
+                source = jnp.concatenate([picked_ref[0, place, :], picked_ref[1, place, :]], axis=0)
+                total += lax.dot_general(
+                    source.astype(jnp.bfloat16),
+                    blocks_ref[tile, k],
+                    NT,
+                    preferred_element_type=jnp.float32,
+                )
+            rows.append(total)
+        for c in range(2):
+            near_ref[c, pl.ds(pl.multiple_of(step * 8, 8), 8), :] = jnp.concatenate(
+                [row[c : c + 1] for row in rows], axis=0
+            )
 
 
 def split(value):
@@ -158,30 +201,120 @@
 
     tile_dev = flow_ref.shape[1]
     rank = basis_ref.shape[0] // tile_dev
-    width = 512
-    for start in range(0, basis_ref.shape[0], width):
-        basis = basis_ref[start : start + width, :]
-        own = lax.broadcasted_iota(jnp.int32, (tile_dev, width), 0) == (
-            lax.broadcasted_iota(jnp.int32, (tile_dev, width), 1) + start
-        ) // rank
+    flows = jnp.concatenate([flow_ref[0], flow_ref[1]], axis=0).astype(jnp.bfloat16)
+    part = 8
+    total = jnp.zeros((rank, 2 * tile_dev), jnp.float32)
+    for start in range(0, tile_dev, part):
+        crossed = lax.dot_general(
+            basis_ref[start * rank : (start + part) * rank, :],
+            flows,
+            NT,
+            preferred_element_type=jnp.float32,
+        )
+        lane = lax.broadcasted_iota(jnp.int32, (rank, 2 * tile_dev), 1) & (tile_dev - 1)
+        for j in range(part):
+            total += jnp.where(lane == start + j, crossed[j * rank : (j + 1) * rank], 0.0)
+    coeff_ref[...] = total.astype(jnp.bfloat16)
+
+
+def far_and_collect_kernel(
+    peers,
+    rows,
+    coeff_ref,
+    admissible_ref,
+    coupling_ref,
+    basis_ref,
+    near_ref,
+    flow_ref,
+    resistance_ref,
+    entry_ref,
+    sign_ref,
+    o_ref,
+    picked_ref,
+    voltage_ref,
+):
+    tile_dev, rank = basis_ref.shape[:2]
+    far_count = coupling_ref.shape[1] // rank
+    group = LANES // far_count
+    held = coeff_ref[...].reshape(peers * rank, 2 * tile_dev)
+    for start in range(0, admissible_ref.shape[1], 512):
+        index = admissible_ref[:, start : start + 512]
+        low = index & (tile_dev - 1)
+        owner = index // tile_dev
+        tile = lax.broadcasted_iota(jnp.int32, (2 * tile_dev, 512), 0)
         for c in range(2):
-            crossed = lax.dot_general(
-                flow_ref[c].astype(jnp.bfloat16), basis, NT, preferred_element_type=jnp.float32
+            hot = jnp.where(tile == low + c * tile_dev, 1.0, 0.0).astype(jnp.bfloat16)
+            found = jnp.dot(held, hot, preferred_element_type=jnp.float32)
+            total = jnp.zeros((rank, 512), jnp.float32)
+            for p in range(peers):
+                total += jnp.where(owner == p, found[p * rank : (p + 1) * rank], 0.0)
+            for j in range(512 // LANES):
+                picked_ref[start // LANES + j, :, c * LANES : (c + 1) * LANES] = total[
+                    :, j * LANES : (j + 1) * LANES
+                ].astype(jnp.bfloat16)
+    spread = jnp.where(
+        lax.broadcasted_iota(jnp.int32, (2 * LANES, group * LANES), 0) % LANES // far_count
+        == lax.broadcasted_iota(jnp.int32, (2 * LANES, group * LANES), 1) // LANES,
+        1.0,
+        0.0,
+    ).astype(jnp.bfloat16)
+
+    @pl.loop(0, tile_dev // group)
+    def _(step):
+        picked = picked_ref[step]
+        lane = lax.broadcasted_iota(jnp.int32, (rank, 2 * LANES), 1) & (LANES - 1)
+        mixed = jnp.zeros((rank, 2 * LANES), jnp.float32)
+        for j in range(group):
+            crossed = jnp.dot(
+                coupling_ref[step * group + j], picked, preferred_element_type=jnp.float32
             )
-            coeff_ref[c : c + 1, start : start + width] = jnp.sum(
-                jnp.where(own, crossed, 0.0), axis=0, keepdims=True
+            for k in range(far_count):
+                mixed += jnp.where(
+                    lane == j * far_count + k, crossed[k * rank : (k + 1) * rank], 0.0
+                )
+        far = []
+        for c in range(2):
+            wide = jnp.dot(
+                lookup_operand([mixed[:, c * LANES : (c + 1) * LANES]]),
+                spread,
+                preferred_element_type=jnp.float32,
             )
-
-
-def collect_kernel(rows, voltage_ref, entry_ref, sign_ref, o_ref):
+            wide = wide.astype(jnp.bfloat16).astype(jnp.float32)
+            far.append(
+                jnp.concatenate(
+                    [
+                        jnp.sum(
+                            basis_ref[step * group + j].astype(jnp.float32)
+                            * wide[:, j * LANES : (j + 1) * LANES],
+                            axis=0,
+                            keepdims=True,
+                        )
+                        for j in range(group)
+                    ],
+                    axis=0,
+                )
+            )
+        place = pl.ds(pl.multiple_of(step * group, group), group)
+        resistance = resistance_ref[place, :]
+        reactive = [near_ref[c, place, :] + far[c] for c in range(2)]
+        voltage_ref[0, place, :] = resistance * flow_ref[0, place, :] - reactive[1]
+        voltage_ref[1, place, :] = resistance * flow_ref[1, place, :] + reactive[0]
+
     o_ref[...] = jnp.zeros_like(o_ref)
 
     @pl.loop(0, entry_ref.shape[1] // CHUNK)
     def _(step):
         columns = pl.ds(pl.multiple_of(step * CHUNK, CHUNK), CHUNK)
+        tiles = CHUNK // LANES
+        voltage = [
+            voltage_ref[c, pl.ds(pl.multiple_of(step * tiles, tiles), tiles), :] for c in range(2)
+        ]
+        voltage = [
+            jnp.concatenate([value[j : j + 1] for j in range(tiles)], axis=1) for value in voltage
+        ]
         for k in range(entry_ref.shape[0]):
             orient = (2 * sign_ref[k : k + 1, columns] - 1).astype(jnp.float32)
-            values = [orient * voltage_ref[c : c + 1, columns] for c in range(2)]
+            values = [orient * voltage[c] for c in range(2)]
             o_ref[...] += sums(values, entry_ref[k : k + 1, columns], rows)
 
 
@@ -211,10 +344,11 @@
         o_ref[c] = sums_ref[c * rows : c * rows + mesh_rows, :] + arrived[own] + ports[own]
 
 
-def local_call(body, shapes, *arrays):
+def local_call(body, shapes, *arrays, scratch=()):
     return pl.pallas_call(
         body,
         out_shape=shapes,
+        scratch_shapes=list(scratch),
         compiler_params=pltpu.CompilerParams(vmem_limit_bytes=VMEM_LIMIT),
     )(*arrays)
 
@@ -240,7 +374,6 @@
 ):
     peers = lax.axis_size("clus")
     mesh_dev = mesh_current.shape[1]
-    branch_dev = branch_entry.shape[1]
     tile_dev, near_count, tile_width = near_blocks.shape[:3]
     rank = basis_in.shape[1]
     ports = port_mesh.shape[0]
@@ -265,45 +398,40 @@
     )
     flow, coeff = local_call(
         functools.partial(branch_kernel, peers, rows),
-        [f32(2, tile_dev, LANES), f32(2, tile_dev * rank)],
+        [f32(2, tile_dev, LANES), jax.ShapeDtypeStruct((rank, 2 * tile_dev), jnp.bfloat16)],
         current,
         answer,
         branch_entry,
         branch_sign,
         basis_in.reshape(tile_dev * rank, tile_width),
     )
-    branch_input = flow.astype(jnp.bfloat16)
-    mine = coeff.astype(jnp.bfloat16).reshape(-1, LANES)
-    all_coeff = exchange(mine, peers, 2, gather=True)
-
-    near_hot = jax.nn.one_hot(near_source.reshape(-1), tile_dev, dtype=jnp.bfloat16)
-    near_input = jnp.einsum(
-        "ns,csj->cnj", near_hot, branch_input, preferred_element_type=jnp.bfloat16
-    ).reshape(2, tile_dev, near_count, tile_width)
-    near_field = jnp.einsum(
-        "tkij,ctkj->cti", near_blocks, near_input, preferred_element_type=jnp.float32
-    )
-    table = all_coeff.reshape(peers, 2, tile_dev, rank).transpose(0, 2, 1, 3)
-    far_hot = jax.nn.one_hot(admissible.reshape(-1), peers * tile_dev, dtype=jnp.bfloat16)
-    picked = jnp.dot(
-        far_hot,
-        table.reshape(peers * tile_dev, 2 * rank),
-        preferred_element_type=jnp.bfloat16,
-    ).reshape(tile_dev, -1, 2, rank)
-    far_mixed = jnp.einsum(
-        "tkrq,tkcq->ctr", coupling, picked, preferred_element_type=jnp.float32
-    ).astype(jnp.bfloat16)
-    far_field = jnp.einsum("tri,ctr->cti", basis_out, far_mixed, preferred_element_type=jnp.float32)
-    reactive = near_field + far_field
-    resistive = resistance.reshape(1, tile_dev, tile_width) * flow
-    voltage = (resistive + jnp.stack([-reactive[1], reactive[0]])).reshape(2, branch_dev)
-
+    all_coeff, near_field = exchange(
+        coeff,
+        peers,
+        2,
+        gather=True,
+        work=near_work,
+        extra=(flow, near_source.reshape(-1, 1), near_blocks),
+        made=(f32(2, tile_dev, LANES),),
+        scratch=(pltpu.VMEM((2, tile_dev * near_count, LANES), jnp.float32),),
+    )
+    far_count = admissible.shape[1]
     totals = local_call(
-        functools.partial(collect_kernel, rows),
+        functools.partial(far_and_collect_kernel, peers, rows),
         f32(2 * rows, LANES),
-        voltage,
+        all_coeff,
+        admissible.reshape(1, -1),
+        coupling.reshape(tile_dev, far_count * rank, rank),
+        basis_out,
+        near_field,
+        flow,
+        resistance.reshape(tile_dev, tile_width),
         branch_entry,
         branch_sign,
+        scratch=(
+            pltpu.VMEM((tile_dev * far_count // LANES, rank, 2 * LANES), jnp.bfloat16),
+            pltpu.VMEM((2, tile_dev, LANES), jnp.float32),
+        ),
     )
     slots = totals.reshape(2, rows, LANES)[:, mesh_rows:].transpose(1, 0, 2)
     arrived = exchange(jnp.pad(slots, ((0, 0), (0, 6), (0, 0))), peers, 3)

time: 86.2 us -> 76.8 us (0.89)
  matrix products: 12 us -> 0 us
  Pallas kernels: 44 us -> 56 us
  local copies, waits for them, and re-layouts: 28.4 us -> 19.4 us
    dot_general x4 -> x0, matrix products: 12 us -> none  [the longest x1 5.68 us: per_device(): jnp.einsum('tkij,ctkj->cti', near_blocks, near_input, preferred_element_t...]
    pallas_call x8, Pallas kernels: 44 us -> 56 us  [the longest x4 36.4 us: exchange(): pl.pallas_call(functools.partial(exchange_kernel, peers, gather, work), o...]
    unnamed x37 -> x24, local copies, waits for them, and re-layouts: 23.9 us -> 18.5 us
    reshape x3 -> x2, local copies, waits for them, and re-layouts: 1.95 us -> 0.17 us  [the longest x1 0.09 us: per_device(): admissible.reshape(1, -1)]
where the time goes in v2:
time: 76.8 us; the launch traced here: 76.2 us
  Pallas kernels  56 us (73%)
  local copies, waits for them, and re-layouts  19.4 us (25%)
    pallas_call x4, Pallas kernels, exchange(): pl.pallas_call(functools.partial(exchange_kernel, peers, gather, work), o...  36.4 us
    pallas_call x4, Pallas kernels, local_call(): pl.pallas_call(body, out_shape=shapes, scratch_shapes=list(scratch), comp...  19.6 us
    unnamed x24, local copies, waits for them, and re-layouts  18.5 us

profile of v2, /device:TPU:0, one launch (start us, length us, event | category | flops | bytes accessed | tf_op | source)
XLA Modules:
  0.0 76.2 jit_solution(13267939808487464294)
XLA Ops:
  0.0 0.7 pad.16.x_ref
  0.7 9.0 %shard_map.127.asked_ref = s32[16,8,128]{2,1,0:T(8,128)S(1)} custom-call(s32[16,8,128]{2,1,0:T(8,128)S(1)} %pad.16.x_ref), custom_call_target="tpu_custom_call" | custom-call | tf_op jit(solution)/shard_map/pallas_call | solution.py:64
  9.7 0.8 %copy.29 = f32[1,2,32,128]{3,2,1,0:T(8,128)S(1)} copy(f32[1,2,32,128]{3,1,2,0:T(2,128)} %bitcast.26) | data formatting | bytes 65536
  10.5 0.7 subtract_bitcast_fusion.port_ref
  11.1 0.4 shard_map.128.x_ref
  11.5 7.1 %shard_map.129.remote_ref.answer_ref = f32[16,8,128]{2,1,0:T(8,128)S(1)} custom-call(f32[16,8,128]{2,1,0:T(8,128)S(1)} %shard_map.128.x_ref), custom_call_target="tpu_custom_call" | custom-call | tf_op jit(solution)/shard_map/pallas_call | solution.py:64
  18.6 0.0 copy-start.1
  18.6 1.0 %copy-done.1 = bf16[64,32,128]{2,1,0:T(8,128)(2,1)S(1)} copy-done((bf16[64,32,128]{2,1,0:T(8,128)(2,1)S(1)}, bf16[64,32,128]{2,1,0:T(8,128)(2,1)}, u32[]{:S(2)}) %copy-start.1) | copy-done | bytes 524312
  19.6 0.8 %copy-done.2 = s32[2,8192]{1,0:T(2,128)S(1)} copy-done((s32[2,8192]{1,0:T(2,128)S(1)}, s32[2,8192]{1,0:T(2,128)}, u32[]{:S(2)}) %copy-start.2) | copy-done | bytes 65560
  20.5 0.8 %copy-done.4 = s32[2,8192]{1,0:T(2,128)S(1)} copy-done((s32[2,8192]{1,0:T(2,128)S(1)}, s32[2,8192]{1,0:T(2,128)}, u32[]{:S(2)}) %copy-start.4) | copy-done | bytes 65560
  21.3 3.2 %shard_map.130 = (f32[2,64,128]{2,1,0:T(8,128)S(1)}, bf16[32,128]{1,0:T(8,128)(2,1)S(1)}) custom-call(f32[2,32,128]{2,1,0:T(8,128)S(1)} %bitcast.20, f32[16,8,128]{2,1,0:T(8,128)S(1)} %shard_map.129.remote_ref.answer_ref, s32[2,8192]{1,0:T(2,128)S(1)} %copy-done.2, s32[2,8192]{1,0:T(2,128)S(1)} %copy-done.4, bf16[2048,128]{1,0:T(8,128)(2,1)S(1)} %bitcast.18), custom_call_target="tpu_custom_call" | custom-call | tf_op jit(solution)/shard_map/pallas_call | solution.py:348
  24.6 0.8 %copy.17 = s32[64,4]{1,0:T(8,128)S(1)} copy(s32[64,4]{0,1:T(4,128)} %param.19) | data formatting | bytes 2048 | tf_op args[6]
  25.3 0.1 reshape.33.refs_1_
  25.4 13.4 %shard_map.131 = (bf16[16,32,128]{2,1,0:T(8,128)(2,1)S(1)}, f32[2,64,128]{2,1,0:T(8,128)S(1)}) custom-call(bf16[32,128]{1,0:T(8,128)(2,1)S(1)} %get-tuple-element.9.x_ref, f32[2,64,128]{2,1,0:T(8,128)S(1)} %get-tuple-element.10.refs_0_.flow_ref, s32[256,1]{1,0:T(8,128)S(1)} %reshape.33.refs_1_, bf16[64,4,128,128]{3,2,1,0:T(8,128)(2,1)} %refs_2_.1), custom_call_target="tpu_custom_call" | custom-call | tf_op jit(solution)/shard_map/pallas_call | solution.py:64
  38.8 0.0 copy-start.8
  38.8 0.0 copy-start
  38.8 0.0 copy-start.3
  38.8 0.0 copy-start.5
  38.8 0.0 copy-start.6
  38.9 0.0 copy-start.7
  38.9 13.4 %copy.20 = bf16[64,16,32,32]{3,2,1,0:T(8,128)(2,1)} copy(bf16[64,16,32,32]{0,3,2,1:T(8,128)(2,1)} %param.21) | data formatting | bytes 4194304 | tf_op args[8]
  52.2 0.0 copy-done.8
  52.2 0.1 copy.19
  52.3 0.1 reshape.28.admissible_ref
  52.4 0.0 copy-done
  52.4 0.0 copy-done.3
  52.4 0.0 copy-done.5
  52.4 15.4 %shard_map.132.sums_ref = f32[96,128]{1,0:T(8,128)S(1)} custom-call(bf16[16,32,128]{2,1,0:T(8,128)(2,1)S(1)} %get-tuple-element.11.coeff_ref, s32[1,1024]{1,0:T(1,128)S(1)} %reshape.28.admissible_ref, bf16[64,512,32]{2,1,0:T(8,128)(2,1)} %bitcast.24, bf16[64,32,128]{2,1,0:T(8,128)(2,1)S(1)} %copy-done, f32[2,64,128]{2,1,0:T(8,128)S(1)} %get-tuple-element.12.near_ref, ...), custom_call_target="tpu_custom_call" | custom-call | tf_op jit(solution)/shard_map/pallas_call | solution.py:348
  67.9 6.9 %shard_map.133.arrived_ref = f32[16,8,128]{2,1,0:T(8,128)S(1)} custom-call(f32[16,8,128]{2,1,0:T(8,128)S(1)} %pad.18.x_ref), custom_call_target="tpu_custom_call" | custom-call | tf_op jit(solution)/shard_map/pallas_call | solution.py:64
  74.8 0.0 copy-done.7
  74.9 0.6 shard_map.134
  75.5 0.7 copy.28
  (7 shorter events, 0.0 us)
Async XLA Ops:
  18.6 1.0 %copy-start.1 = (bf16[64,32,128]{2,1,0:T(8,128)(2,1)S(1)}, bf16[64,32,128]{2,1,0:T(8,128)(2,1)}, u32[]{:S(2)}) copy-start(bf16[64,32,128]{2,1,0:T(8,128)(2,1)} %param.20) | copy-start | bytes 1572868
  19.6 0.8 %copy-start.2 = (s32[2,8192]{1,0:T(2,128)S(1)}, s32[2,8192]{1,0:T(2,128)}, u32[]{:S(2)}) copy-start(s32[2,8192]{1,0:T(2,128)} %entry_ref.3) | copy-start | bytes 196612
  20.5 0.8 %copy-start.4 = (s32[2,8192]{1,0:T(2,128)S(1)}, s32[2,8192]{1,0:T(2,128)}, u32[]{:S(2)}) copy-start(s32[2,8192]{1,0:T(2,128)} %sign_ref.3) | copy-start | bytes 196612
  38.8 13.4 %copy-start.8 = (s32[64,16]{0,1:T(8,128)S(1)}, s32[64,16]{0,1:T(8,128)}, u32[]{:S(2)}) copy-start(s32[64,16]{0,1:T(8,128)} %param.23) | copy-start | bytes 12292
  38.8 13.6 %copy-start = (bf16[64,32,128]{2,1,0:T(8,128)(2,1)S(1)}, bf16[64,32,128]{2,1,0:T(8,128)(2,1)}, u32[]{:S(2)}) copy-start(bf16[64,32,128]{2,1,0:T(8,128)(2,1)} %basis_ref.1) | copy-start | bytes 1572868
  38.8 13.6 %copy-start.3 = (s32[2,8192]{1,0:T(2,128)S(1)}, s32[2,8192]{1,0:T(2,128)}, u32[]{:S(2)}) copy-start(s32[2,8192]{1,0:T(2,128)} %entry_ref.3) | copy-start | bytes 196612
  38.8 13.6 %copy-start.5 = (s32[2,8192]{1,0:T(2,128)S(1)}, s32[2,8192]{1,0:T(2,128)}, u32[]{:S(2)}) copy-start(s32[2,8192]{1,0:T(2,128)} %sign_ref.3) | copy-start | bytes 196612
  38.8 13.6 %copy-start.6 = (f32[8192]{0:T(1024)S(1)}, f32[8192]{0:T(1024)}, u32[]{:S(2)}) copy-start(f32[8192]{0:T(1024)} %param.17) | copy-start | bytes 98308
  38.9 36.0 %copy-start.7 = (f32[2,64,64]{2,1,0:T(8,128)S(1)}, f32[2,64,64]{2,1,0:T(8,128)}, u32[]{:S(2)}) copy-start(f32[2,64,64]{2,1,0:T(8,128)} %param.25) | copy-start | bytes 98308

commit v3 on v2

--- a/solution.py
+++ b/solution.py
@@ -231,11 +231,12 @@
     sign_ref,
     o_ref,
     picked_ref,
+    mixed_ref,
     voltage_ref,
 ):
     tile_dev, rank = basis_ref.shape[:2]
-    far_count = coupling_ref.shape[1] // rank
-    group = LANES // far_count
+    far_count = coupling_ref.shape[0]
+    group = 8
     held = coeff_ref[...].reshape(peers * rank, 2 * tile_dev)
     for start in range(0, admissible_ref.shape[1], 512):
         index = admissible_ref[:, start : start + 512]
@@ -249,33 +250,32 @@
             for p in range(peers):
                 total += jnp.where(owner == p, found[p * rank : (p + 1) * rank], 0.0)
             for j in range(512 // LANES):
-                picked_ref[start // LANES + j, :, c * LANES : (c + 1) * LANES] = total[
-                    :, j * LANES : (j + 1) * LANES
-                ].astype(jnp.bfloat16)
-    spread = jnp.where(
-        lax.broadcasted_iota(jnp.int32, (2 * LANES, group * LANES), 0) % LANES // far_count
-        == lax.broadcasted_iota(jnp.int32, (2 * LANES, group * LANES), 1) // LANES,
-        1.0,
-        0.0,
-    ).astype(jnp.bfloat16)
+                picked_ref[c, start // LANES + j] = total[:, j * LANES : (j + 1) * LANES]
+    mixed_ref[...] = jnp.zeros_like(mixed_ref)
+
+    @pl.loop(0, rank)
+    def _(r):
+        total = [0.0, 0.0]
+        for k in range(far_count):
+            block = coupling_ref[k, r].astype(jnp.float32)
+            total = [total[c] + block * picked_ref[c, k, :, :tile_dev] for c in range(2)]
+        for c in range(2):
+            mixed_ref[pl.ds(c * rank + r, 1), :tile_dev] = jnp.sum(
+                total[c], axis=0, keepdims=True
+            )
 
     @pl.loop(0, tile_dev // group)
     def _(step):
-        picked = picked_ref[step]
-        lane = lax.broadcasted_iota(jnp.int32, (rank, 2 * LANES), 1) & (LANES - 1)
-        mixed = jnp.zeros((rank, 2 * LANES), jnp.float32)
-        for j in range(group):
-            crossed = jnp.dot(
-                coupling_ref[step * group + j], picked, preferred_element_type=jnp.float32
-            )
-            for k in range(far_count):
-                mixed += jnp.where(
-                    lane == j * far_count + k, crossed[k * rank : (k + 1) * rank], 0.0
-                )
+        spread = jnp.where(
+            lax.broadcasted_iota(jnp.int32, (2 * LANES, group * LANES), 0) % LANES - step * group
+            == lax.broadcasted_iota(jnp.int32, (2 * LANES, group * LANES), 1) // LANES,
+            1.0,
+            0.0,
+        ).astype(jnp.bfloat16)
         far = []
         for c in range(2):
             wide = jnp.dot(
-                lookup_operand([mixed[:, c * LANES : (c + 1) * LANES]]),
+                lookup_operand([mixed_ref[c * rank : (c + 1) * rank, :]]),
                 spread,
                 preferred_element_type=jnp.float32,
             )
@@ -420,8 +420,8 @@
         functools.partial(far_and_collect_kernel, peers, rows),
         f32(2 * rows, LANES),
         all_coeff,
-        admissible.reshape(1, -1),
-        coupling.reshape(tile_dev, far_count * rank, rank),
+        jnp.pad(admissible.T, ((0, 0), (0, LANES - tile_dev))).reshape(1, -1),
+        coupling.transpose(1, 2, 3, 0),
         basis_out,
         near_field,
         flow,
@@ -429,7 +429,8 @@
         branch_entry,
         branch_sign,
         scratch=(
-            pltpu.VMEM((tile_dev * far_count // LANES, rank, 2 * LANES), jnp.bfloat16),
+            pltpu.VMEM((2, far_count, rank, LANES), jnp.float32),
+            pltpu.VMEM((2 * rank, LANES), jnp.float32),
             pltpu.VMEM((2, tile_dev, LANES), jnp.float32),
         ),
     )

time: 76.8 us -> 57.2 us (0.74)
  local copies, waits for them, and re-layouts: 19.4 us -> 5.87 us
  Pallas kernels: 56 us -> 50.1 us
    unnamed x24, local copies, waits for them, and re-layouts: 18.5 us -> 4.99 us
    pallas_call x4, Pallas kernels: 19.6 us -> 13.5 us  [local_call(): pl.pallas_call(body, out_shape=shapes, scratch_shapes=list(scratch), comp...]
where the time goes in v3:
time: 57.2 us; the launch traced here: 56.8 us
  Pallas kernels  50.1 us (88%)
  local copies, waits for them, and re-layouts  5.87 us (10%)
  other arithmetic  0.66 us (1%)
    pallas_call x4, Pallas kernels, exchange(): pl.pallas_call(functools.partial(exchange_kernel, peers, gather, work), o...  36.6 us
    pallas_call x4, Pallas kernels, local_call(): pl.pallas_call(body, out_shape=shapes, scratch_shapes=list(scratch), comp...  13.5 us
    unnamed x24, local copies, waits for them, and re-layouts  4.99 us

profile of v3, /device:TPU:0, one launch (start us, length us, event | category | flops | bytes accessed | tf_op | source)
XLA Modules:
  0.0 56.8 jit_solution(15639411420010834160)
XLA Ops:
  0.0 0.0 copy-start.9
  0.0 0.0 copy-start.7
  0.0 0.8 %pad.20.x_ref = s32[16,8,128]{2,1,0:T(8,128)S(1)} pad(s32[16,1,128]{2,1,0:T(1,128)} %bitcast.30, s32[]{:T(128)} %constant.2.clone.1), padding=0_0x0_7x0_0 | pad | bytes 73732 | tf_op jit(solution)/shard_map/jit(_pad)/pad | solution.py:387
  0.8 9.0 %shard_map.127.asked_ref = s32[16,8,128]{2,1,0:T(8,128)S(1)} custom-call(s32[16,8,128]{2,1,0:T(8,128)S(1)} %pad.20.x_ref), custom_call_target="tpu_custom_call" | custom-call | tf_op jit(solution)/shard_map/pallas_call | solution.py:64
  9.8 0.8 %copy.25 = f32[1,2,32,128]{3,2,1,0:T(8,128)S(1)} copy(f32[1,2,32,128]{3,1,2,0:T(2,128)} %bitcast.29) | data formatting | bytes 65536
  10.6 0.7 %subtract_bitcast_fusion.port_ref = s32[1,128]{1,0:T(1,128)S(1)} fusion(s32[64]{0:T(128)} %param.24, s32[]{:T(128)S(6)} %mul.3), kind=kLoop, calls=%fused_computation.3 | loop fusion | flops 128 | bytes 772 | tf_op jit(solution)/shard_map/sub | solution.py:384
  11.2 0.4 shard_map.128.x_ref
  11.6 7.1 %shard_map.129.remote_ref.answer_ref = f32[16,8,128]{2,1,0:T(8,128)S(1)} custom-call(f32[16,8,128]{2,1,0:T(8,128)S(1)} %shard_map.128.x_ref), custom_call_target="tpu_custom_call" | custom-call | tf_op jit(solution)/shard_map/pallas_call | solution.py:64
  18.7 0.0 copy-start.2
  18.7 1.0 %copy-done.2 = bf16[64,32,128]{2,1,0:T(8,128)(2,1)S(1)} copy-done((bf16[64,32,128]{2,1,0:T(8,128)(2,1)S(1)}, bf16[64,32,128]{2,1,0:T(8,128)(2,1)}, u32[]{:S(2)}) %copy-start.2) | copy-done | bytes 524312
  19.7 0.0 copy-start.3
  19.7 0.8 %copy-done.3 = s32[2,8192]{1,0:T(2,128)S(1)} copy-done((s32[2,8192]{1,0:T(2,128)S(1)}, s32[2,8192]{1,0:T(2,128)}, u32[]{:S(2)}) %copy-start.3) | copy-done | bytes 65560
  20.5 0.0 copy-start.5
  20.6 0.8 %copy-done.5 = s32[2,8192]{1,0:T(2,128)S(1)} copy-done((s32[2,8192]{1,0:T(2,128)S(1)}, s32[2,8192]{1,0:T(2,128)}, u32[]{:S(2)}) %copy-start.5) | copy-done | bytes 65560
  21.4 0.0 copy-start.4
  21.4 0.0 copy-start.6
  21.4 3.2 %shard_map.130 = (f32[2,64,128]{2,1,0:T(8,128)S(1)}, bf16[32,128]{1,0:T(8,128)(2,1)S(1)}) custom-call(f32[2,32,128]{2,1,0:T(8,128)S(1)} %bitcast.23, f32[16,8,128]{2,1,0:T(8,128)S(1)} %shard_map.129.remote_ref.answer_ref, s32[2,8192]{1,0:T(2,128)S(1)} %copy-done.3, s32[2,8192]{1,0:T(2,128)S(1)} %copy-done.5, bf16[2048,128]{1,0:T(8,128)(2,1)S(1)} %bitcast.21), custom_call_target="tpu_custom_call" | custom-call | tf_op jit(solution)/shard_map/pallas_call | solution.py:348
  24.6 0.8 %copy.15 = s32[64,4]{1,0:T(8,128)S(1)} copy(s32[64,4]{0,1:T(4,128)} %param.19) | data formatting | bytes 2048 | tf_op args[6]
  25.4 0.1 reshape.29.refs_1_
  25.5 0.0 copy-start
  25.5 13.5 %shard_map.131 = (bf16[16,32,128]{2,1,0:T(8,128)(2,1)S(1)}, f32[2,64,128]{2,1,0:T(8,128)S(1)}) custom-call(bf16[32,128]{1,0:T(8,128)(2,1)S(1)} %get-tuple-element.9.x_ref, f32[2,64,128]{2,1,0:T(8,128)S(1)} %get-tuple-element.10.refs_0_.flow_ref, s32[256,1]{1,0:T(8,128)S(1)} %reshape.29.refs_1_, bf16[64,4,128,128]{3,2,1,0:T(8,128)(2,1)} %refs_2_.1), custom_call_target="tpu_custom_call" | custom-call | tf_op jit(solution)/shard_map/pallas_call | solution.py:64
  39.0 0.0 copy-done.9
  39.1 0.0 copy-done.7
  39.1 0.0 copy-done.1
  39.1 0.0 copy-done.4
  39.1 0.0 copy-done.6
  39.1 0.0 copy-done
  39.1 9.4 %shard_map.132.sums_ref = f32[96,128]{1,0:T(8,128)S(1)} custom-call(bf16[16,32,128]{2,1,0:T(8,128)(2,1)S(1)} %get-tuple-element.11.coeff_ref, s32[1,2048]{1,0:T(1,128)S(1)} %bitcast.27, bf16[16,32,32,64]{3,2,1,0:T(8,128)(2,1)S(1)} %bitcast.20, bf16[64,32,128]{2,1,0:T(8,128)(2,1)S(1)} %copy-done.1, f32[2,64,128]{2,1,0:T(8,128)S(1)} %get-tuple-element.12.near_ref, ...), custom_call_target="tpu_custom_call" | custom-call | tf_op jit(solution)/shard_map/pallas_call | solution.py:348
  48.5 6.9 %shard_map.133.arrived_ref = f32[16,8,128]{2,1,0:T(8,128)S(1)} custom-call(f32[16,8,128]{2,1,0:T(8,128)S(1)} %pad.23.x_ref), custom_call_target="tpu_custom_call" | custom-call | tf_op jit(solution)/shard_map/pallas_call | solution.py:64
  55.5 0.0 copy-done.8
  55.5 0.6 %shard_map.134 = f32[2,32,128]{2,1,0:T(8,128)S(1)} custom-call(f32[96,128]{1,0:T(8,128)S(1)} %shard_map.132.sums_ref, f32[16,8,128]{2,1,0:T(8,128)S(1)} %shard_map.133.arrived_ref, s32[16,8,128]{2,1,0:T(8,128)S(1)} %shard_map.127.asked_ref, f32[16,8,128]{2,1,0:T(8,128)S(1)} %shard_map.129.remote_ref.answer_ref, s32[1,128]{1,0:T(1,128)S(1)} %subtract_bitcast_fusion.port_ref, ...), custom_call_target="tpu_custom_call" | custom-call | tf_op jit(solution)/shard_map/pallas_call | solution.py:348
  56.1 0.7 %copy.24 = f32[1,2,32,128]{3,1,2,0:T(2,128)} copy(f32[1,2,32,128]{3,2,1,0:T(8,128)S(1)} %bitcast.25) | data formatting | bytes 65536
  (7 shorter events, 0.0 us)
Async XLA Ops:
  0.0 39.0 %copy-start.9 = (s32[64,16]{0,1:T(8,128)S(1)}, s32[64,16]{0,1:T(8,128)}, u32[]{:S(2)}) copy-start(s32[64,16]{0,1:T(8,128)} %param.23) | copy-start | bytes 12292
  0.0 39.1 %copy-start.7 = (f32[8192]{0:T(1024)S(1)}, f32[8192]{0:T(1024)}, u32[]{:S(2)}) copy-start(f32[8192]{0:T(1024)} %param.17) | copy-start | bytes 98308
  0.0 39.1 %copy-start.1 = (bf16[64,32,128]{2,1,0:T(8,128)(2,1)S(1)}, bf16[64,32,128]{2,1,0:T(8,128)(2,1)}, u32[]{:S(2)}) copy-start(bf16[64,32,128]{2,1,0:T(8,128)(2,1)} %basis_ref.1) | copy-start | bytes 1572868
  18.7 1.0 %copy-start.2 = (bf16[64,32,128]{2,1,0:T(8,128)(2,1)S(1)}, bf16[64,32,128]{2,1,0:T(8,128)(2,1)}, u32[]{:S(2)}) copy-start(bf16[64,32,128]{2,1,0:T(8,128)(2,1)} %param.20) | copy-start | bytes 1572868
  19.7 0.8 %copy-start.3 = (s32[2,8192]{1,0:T(2,128)S(1)}, s32[2,8192]{1,0:T(2,128)}, u32[]{:S(2)}) copy-start(s32[2,8192]{1,0:T(2,128)} %entry_ref.3) | copy-start | bytes 196612
  20.5 0.8 %copy-start.5 = (s32[2,8192]{1,0:T(2,128)S(1)}, s32[2,8192]{1,0:T(2,128)}, u32[]{:S(2)}) copy-start(s32[2,8192]{1,0:T(2,128)} %sign_ref.3) | copy-start | bytes 196612
  21.4 17.7 %copy-start.4 = (s32[2,8192]{1,0:T(2,128)S(1)}, s32[2,8192]{1,0:T(2,128)}, u32[]{:S(2)}) copy-start(s32[2,8192]{1,0:T(2,128)} %entry_ref.3) | copy-start | bytes 196612
  21.4 17.7 %copy-start.6 = (s32[2,8192]{1,0:T(2,128)S(1)}, s32[2,8192]{1,0:T(2,128)}, u32[]{:S(2)}) copy-start(s32[2,8192]{1,0:T(2,128)} %sign_ref.3) | copy-start | bytes 196612
  21.4 34.1 %copy-start.8 = (f32[2,64,64]{2,1,0:T(8,128)S(1)}, f32[2,64,64]{2,1,0:T(8,128)}, u32[]{:S(2)}) copy-start(f32[2,64,64]{2,1,0:T(8,128)} %param.25) | copy-start | bytes 98308
  25.5 13.6 %copy-start = (bf16[64,16,32,32]{0,3,2,1:T(8,128)(2,1)S(1)}, bf16[64,16,32,32]{0,3,2,1:T(8,128)(2,1)}, u32[]{:S(2)}) copy-start(bf16[64,16,32,32]{0,3,2,1:T(8,128)(2,1)} %param.21) | copy-start | bytes 6291460

commit v4 on v3

--- a/solution.py
+++ b/solution.py
@@ -13,70 +13,51 @@
 NT = (((1,), (1,)), ((), ()))
 
 
-def exchange_kernel(peers, gather, work, x_ref, *refs):
-    *work_ins, o_ref, send_sem, recv_sem, own_sem = refs
-    if work is not None:
-        *work_ins, o_ref, work_out, send_sem, recv_sem, own_sem, work_scratch = refs
+def greet(peers):
     me = lax.axis_index("clus")
-
-    def peer_at(step):
-        return lax.rem(me + step, peers)
+    barrier = pltpu.get_barrier_semaphore()
+
+    @pl.loop(1, peers)
+    def _(step):
+        pl.semaphore_signal(
+            barrier,
+            inc=1,
+            device_id={"clus": lax.rem(me + step, peers)},
+            device_id_type=pl.DeviceIdType.MESH,
+        )
+
+    pl.semaphore_wait(barrier, peers - 1)
+
+
+def push(peers, phase, x_ref, o_ref, send_sem, recv_sem, own_sem, gather=False):
+    me = lax.axis_index("clus")
 
     def copy_at(step):
-        peer = peer_at(step)
+        peer = lax.rem(me + step, peers)
         return pltpu.make_async_remote_copy(
             src_ref=x_ref if gather else x_ref.at[peer],
             dst_ref=o_ref.at[me],
-            send_sem=send_sem.at[step],
-            recv_sem=recv_sem.at[step],
+            send_sem=send_sem.at[phase, step],
+            recv_sem=recv_sem.at[phase, step],
             device_id={"clus": peer},
             device_id_type=pl.DeviceIdType.MESH,
         )
 
-    barrier = pltpu.get_barrier_semaphore()
-
-    @pl.loop(1, peers)
-    def _(step):
-        pl.semaphore_signal(
-            barrier, inc=1, device_id={"clus": peer_at(step)}, device_id_type=pl.DeviceIdType.MESH
-        )
-
-    own = pltpu.make_async_copy(x_ref if gather else x_ref.at[me], o_ref.at[me], own_sem)
-    own.start()
-    pl.semaphore_wait(barrier, peers - 1)
-
     @pl.loop(1, peers)
     def _(step):
         copy_at(step).start()
 
-    own.wait()
-    if work is not None:
-        work(*work_ins, work_out, work_scratch)
-
-    @pl.loop(1, peers)
-    def _(step):
-        copy_at(step).wait()
-
-
-def exchange(x, peers, collective_id, gather=False, work=None, extra=(), made=(), scratch=()):
-    shape = (peers,) + (x.shape if gather else x.shape[1:])
-    vmem = pl.BlockSpec(memory_space=pltpu.VMEM)
-    out = pl.pallas_call(
-        functools.partial(exchange_kernel, peers, gather, work),
-        out_shape=[jax.ShapeDtypeStruct(shape, x.dtype), *made],
-        in_specs=[vmem] * (1 + len(extra)),
-        out_specs=[vmem] * (1 + len(made)),
-        scratch_shapes=[
-            pltpu.SemaphoreType.DMA((peers,)),
-            pltpu.SemaphoreType.DMA((peers,)),
-            pltpu.SemaphoreType.DMA,
-            *scratch,
-        ],
-        compiler_params=pltpu.CompilerParams(
-            collective_id=collective_id, has_side_effects=True, vmem_limit_bytes=VMEM_LIMIT
-        ),
-    )(x, *extra)
-    return out if made else out[0]
+    own = pltpu.make_async_copy(x_ref if gather else x_ref.at[me], o_ref.at[me], own_sem.at[phase])
+    own.start()
+
+    def finish():
+        own.wait()
+
+        @pl.loop(1, peers)
+        def _(step):
+            copy_at(step).wait()
+
+    return finish
 
 
 def near_work(flow_ref, source_ref, blocks_ref, near_ref, picked_ref):
@@ -344,13 +325,97 @@
         o_ref[c] = sums_ref[c * rows : c * rows + mesh_rows, :] + arrived[own] + ports[own]
 
 
-def local_call(body, shapes, *arrays, scratch=()):
-    return pl.pallas_call(
-        body,
-        out_shape=shapes,
-        scratch_shapes=list(scratch),
-        compiler_params=pltpu.CompilerParams(vmem_limit_bytes=VMEM_LIMIT),
-    )(*arrays)
+def whole_kernel(
+    peers,
+    rows,
+    mesh_rows,
+    need_ref,
+    current_ref,
+    port_ref,
+    entry_ref,
+    sign_ref,
+    basis_in_ref,
+    source_ref,
+    blocks_hbm,
+    admissible_ref,
+    coupling_hbm,
+    basis_out_ref,
+    resistance_ref,
+    z_ref,
+    o_ref,
+    asked_ref,
+    reply_ref,
+    answer_ref,
+    flow_ref,
+    coeff_ref,
+    all_coeff_ref,
+    blocks_ref,
+    coupling_ref,
+    near_ref,
+    near_picked_ref,
+    picked_ref,
+    mixed_ref,
+    voltage_ref,
+    totals_ref,
+    slots_ref,
+    arrived_ref,
+    send_sem,
+    recv_sem,
+    own_sem,
+    load_sem,
+):
+    load_blocks = pltpu.make_async_copy(blocks_hbm, blocks_ref, load_sem.at[0])
+    load_coupling = pltpu.make_async_copy(coupling_hbm, coupling_ref, load_sem.at[1])
+    load_blocks.start()
+    load_coupling.start()
+    sems = (send_sem, recv_sem, own_sem)
+    greet(peers)
+    push(peers, 0, need_ref, asked_ref, *sems)()
+    answer_kernel(peers, mesh_rows, current_ref, asked_ref, port_ref, reply_ref)
+    push(peers, 1, reply_ref, answer_ref, *sems)()
+    branch_kernel(
+        peers, rows, current_ref, answer_ref, entry_ref, sign_ref, basis_in_ref, flow_ref, coeff_ref
+    )
+    finish = push(peers, 2, coeff_ref, all_coeff_ref, *sems, gather=True)
+    load_blocks.wait()
+    near_work(flow_ref, source_ref, blocks_ref, near_ref, near_picked_ref)
+    load_coupling.wait()
+    finish()
+    far_and_collect_kernel(
+        peers,
+        rows,
+        all_coeff_ref,
+        admissible_ref,
+        coupling_ref,
+        basis_out_ref,
+        near_ref,
+        flow_ref,
+        resistance_ref,
+        entry_ref,
+        sign_ref,
+        totals_ref,
+        picked_ref,
+        mixed_ref,
+        voltage_ref,
+    )
+    slots_ref[...] = jnp.zeros_like(slots_ref)
+    for p in range(peers):
+        for c in range(2):
+            row = c * rows + mesh_rows + p
+            slots_ref[p, c : c + 1, :] = totals_ref[row : row + 1, :]
+    push(peers, 3, slots_ref, arrived_ref, *sems)()
+    finish_kernel(
+        peers,
+        rows,
+        mesh_rows,
+        totals_ref,
+        arrived_ref,
+        asked_ref,
+        answer_ref,
+        port_ref,
+        z_ref,
+        o_ref,
+    )
 
 
 def f32(*shape):
@@ -384,66 +449,54 @@
     port_position = jnp.pad(port_mesh, (0, LANES - ports), constant_values=-1)[None, :] - offset
     impedance = jnp.pad(port_coupling, ((0, 0), (0, LANES - ports), (0, LANES - ports)))
 
-    asked = exchange(jnp.pad(need_slots[:, None, :], ((0, 0), (0, 7), (0, 0))), peers, 0)
-    answer = exchange(
-        local_call(
-            functools.partial(answer_kernel, peers, mesh_rows),
-            f32(peers, 8, LANES),
-            current,
-            asked,
-            port_position,
+    far_count = admissible.shape[1]
+    vmem, hbm = pl.BlockSpec(memory_space=pltpu.VMEM), pl.BlockSpec(memory_space=pl.ANY)
+    mixing = coupling.transpose(1, 2, 3, 0)
+    message = pltpu.VMEM((peers, 8, LANES), jnp.float32)
+    tiles = pltpu.VMEM((2, tile_dev, LANES), jnp.float32)
+    made = pl.pallas_call(
+        functools.partial(whole_kernel, peers, rows, mesh_rows),
+        out_shape=f32(2, mesh_rows, LANES),
+        in_specs=[vmem] * 7 + [hbm, vmem, hbm] + [vmem] * 3,
+        out_specs=vmem,
+        scratch_shapes=[
+            pltpu.VMEM((peers, 8, LANES), jnp.int32),
+            message,
+            message,
+            tiles,
+            pltpu.VMEM((rank, 2 * tile_dev), jnp.bfloat16),
+            pltpu.VMEM((peers, rank, 2 * tile_dev), jnp.bfloat16),
+            pltpu.VMEM(near_blocks.shape, near_blocks.dtype),
+            pltpu.VMEM(mixing.shape, mixing.dtype),
+            tiles,
+            pltpu.VMEM((2, tile_dev * near_count, LANES), jnp.float32),
+            pltpu.VMEM((2, far_count, rank, LANES), jnp.float32),
+            pltpu.VMEM((2 * rank, LANES), jnp.float32),
+            tiles,
+            pltpu.VMEM((2 * rows, LANES), jnp.float32),
+            message,
+            message,
+            pltpu.SemaphoreType.DMA((4, peers)),
+            pltpu.SemaphoreType.DMA((4, peers)),
+            pltpu.SemaphoreType.DMA((4,)),
+            pltpu.SemaphoreType.DMA((2,)),
+        ],
+        compiler_params=pltpu.CompilerParams(
+            collective_id=0, has_side_effects=True, vmem_limit_bytes=VMEM_LIMIT
         ),
-        peers,
-        1,
-    )
-    flow, coeff = local_call(
-        functools.partial(branch_kernel, peers, rows),
-        [f32(2, tile_dev, LANES), jax.ShapeDtypeStruct((rank, 2 * tile_dev), jnp.bfloat16)],
+    )(
+        jnp.pad(need_slots[:, None, :], ((0, 0), (0, 7), (0, 0))),
         current,
-        answer,
+        port_position,
         branch_entry,
         branch_sign,
         basis_in.reshape(tile_dev * rank, tile_width),
-    )
-    all_coeff, near_field = exchange(
-        coeff,
-        peers,
-        2,
-        gather=True,
-        work=near_work,
-        extra=(flow, near_source.reshape(-1, 1), near_blocks),
-        made=(f32(2, tile_dev, LANES),),
-        scratch=(pltpu.VMEM((2, tile_dev * near_count, LANES), jnp.float32),),
-    )
-    far_count = admissible.shape[1]
-    totals = local_call(
-        functools.partial(far_and_collect_kernel, peers, rows),
-        f32(2 * rows, LANES),
-        all_coeff,
+        near_source.reshape(-1, 1),
+        near_blocks,
         jnp.pad(admissible.T, ((0, 0), (0, LANES - tile_dev))).reshape(1, -1),
-        coupling.transpose(1, 2, 3, 0),
+        mixing,
         basis_out,
-        near_field,
-        flow,
         resistance.reshape(tile_dev, tile_width),
-        branch_entry,
-        branch_sign,
-        scratch=(
-            pltpu.VMEM((2, far_count, rank, LANES), jnp.float32),
-            pltpu.VMEM((2 * rank, LANES), jnp.float32),
-            pltpu.VMEM((2, tile_dev, LANES), jnp.float32),
-        ),
-    )
-    slots = totals.reshape(2, rows, LANES)[:, mesh_rows:].transpose(1, 0, 2)
-    arrived = exchange(jnp.pad(slots, ((0, 0), (0, 6), (0, 0))), peers, 3)
-    made = local_call(
-        functools.partial(finish_kernel, peers, rows, mesh_rows),
-        f32(2, mesh_rows, LANES),
-        totals,
-        arrived,
-        asked,
-        answer,
-        port_position,
         impedance,
     )
     return made.reshape(2, mesh_dev)

time: 57.2 us -> 51.2 us (0.90)
  Pallas kernels: 50.1 us -> 38.7 us
  local copies, waits for them, and re-layouts: 5.87 us -> 11.2 us
    pallas_call x8 -> x1, Pallas kernels: 50.1 us -> 38.7 us  [per_device(): pl.pallas_call(functools.partial(whole_kernel, peers, rows, mesh_rows), o...]
    unnamed x24 -> x15, local copies, waits for them, and re-layouts: 4.99 us -> 8.87 us
    pad x1, local copies, waits for them, and re-layouts: 0.01 us -> 0.86 us  [per_device(): jnp.pad(port_coupling, ((0, 0), (0, LANES - ports), (0, LANES - ports)))]
    pad x1, local copies, waits for them, and re-layouts: 0.01 us -> 0.7 us  [per_device(): jnp.pad(admissible.T, ((0, 0), (0, LANES - tile_dev))).reshape(1, -1)]
where the time goes in v4:
time: 51.2 us; the launch traced here: 50.6 us
  Pallas kernels  38.7 us (76%)
  local copies, waits for them, and re-layouts  11.2 us (22%)
  other arithmetic  0.66 us (1%)
    pallas_call x1, Pallas kernels, per_device(): pl.pallas_call(functools.partial(whole_kernel, peers, rows, mesh_rows), o...  38.7 us
    unnamed x15, local copies, waits for them, and re-layouts  8.87 us

profile of v4, /device:TPU:0, one launch (start us, length us, event | category | flops | bytes accessed | tf_op | source)
XLA Modules:
  0.0 50.6 jit_solution(6675419821807920594)
XLA Ops:
  0.0 0.7 %subtract_bitcast_fusion.port_ref = s32[1,128]{1,0:T(1,128)S(1)} fusion(s32[64]{0:T(128)} %param.24, s32[]{:T(128)S(6)} %mul.3), kind=kLoop, calls=%fused_computation.2 | loop fusion | flops 128 | bytes 772 | tf_op jit(solution)/shard_map/sub | solution.py:449
  0.7 0.7 %pad.18 = s32[16,128]{1,0:T(8,128)S(1)} pad(s32[16,64]{1,0:T(8,128)} %bitcast.24, s32[]{:T(128)} %constant.2.clone.1), padding=0_0x0_64 | pad | bytes 12292 | tf_op jit(solution)/shard_map/jit(_pad)/pad | solution.py:496
  1.4 0.8 %copy.22 = f32[1,2,32,128]{3,2,1,0:T(8,128)S(1)} copy(f32[1,2,32,128]{3,1,2,0:T(2,128)} %bitcast.22) | data formatting | bytes 65536
  2.1 0.8 %copy.15 = s32[64,4]{1,0:T(8,128)S(1)} copy(s32[64,4]{0,1:T(4,128)} %param.19) | data formatting | bytes 2048 | tf_op args[6]
  2.9 0.7 %pad.16.need_ref = s32[16,8,128]{2,1,0:T(8,128)S(1)} pad(s32[16,1,128]{2,1,0:T(1,128)} %bitcast.23, s32[]{:T(128)} %constant.2.clone.1), padding=0_0x0_7x0_0 | pad | bytes 73732 | tf_op jit(solution)/shard_map/jit(_pad)/pad | solution.py:488
  3.6 0.1 reshape.25.source_ref
  3.7 0.9 %pad.19.z_ref = f32[2,128,128]{2,1,0:T(8,128)S(1)} pad(f32[2,64,64]{2,1,0:T(8,128)} %param.25, f32[]{:T(128)} %constant.11.clone.1), padding=0_0x0_64x0_64 | pad | bytes 163844 | tf_op jit(solution)/shard_map/jit(_pad)/pad | solution.py:450
  4.5 0.0 copy-start
  4.6 2.2 %copy-done = bf16[64,16,32,32]{0,3,2,1:T(8,128)(2,1)S(1)} copy-done((bf16[64,16,32,32]{0,3,2,1:T(8,128)(2,1)S(1)}, bf16[64,16,32,32]{0,3,2,1:T(8,128)(2,1)}, u32[]{:S(2)}) %copy-start) | copy-done | bytes 2097176
  6.7 0.0 copy-start.1
  6.7 1.0 %copy-done.1 = bf16[64,32,128]{2,1,0:T(8,128)(2,1)S(1)} copy-done((bf16[64,32,128]{2,1,0:T(8,128)(2,1)S(1)}, bf16[64,32,128]{2,1,0:T(8,128)(2,1)}, u32[]{:S(2)}) %copy-start.1) | copy-done | bytes 524312
  7.8 0.0 copy-start.2
  7.8 1.0 %copy-done.2 = bf16[64,32,128]{2,1,0:T(8,128)(2,1)S(1)} copy-done((bf16[64,32,128]{2,1,0:T(8,128)(2,1)S(1)}, bf16[64,32,128]{2,1,0:T(8,128)(2,1)}, u32[]{:S(2)}) %copy-start.2) | copy-done | bytes 524312
  8.8 0.0 copy-start.3
  8.8 0.8 %copy-done.3 = s32[2,8192]{1,0:T(2,128)S(1)} copy-done((s32[2,8192]{1,0:T(2,128)S(1)}, s32[2,8192]{1,0:T(2,128)}, u32[]{:S(2)}) %copy-start.3) | copy-done | bytes 65560
  9.7 0.0 copy-start.4
  9.7 0.8 %copy-done.4 = s32[2,8192]{1,0:T(2,128)S(1)} copy-done((s32[2,8192]{1,0:T(2,128)S(1)}, s32[2,8192]{1,0:T(2,128)}, u32[]{:S(2)}) %copy-start.4) | copy-done | bytes 65560
  10.5 0.0 copy-start.5
  10.5 0.8 %copy-done.5 = f32[8192]{0:T(1024)S(1)} copy-done((f32[8192]{0:T(1024)S(1)}, f32[8192]{0:T(1024)}, u32[]{:S(2)}) %copy-start.5) | copy-done | bytes 32792
  11.3 38.7 %shard_map.127 = f32[2,32,128]{2,1,0:T(8,128)S(1)} custom-call(s32[16,8,128]{2,1,0:T(8,128)S(1)} %pad.16.need_ref, f32[2,32,128]{2,1,0:T(8,128)S(1)} %bitcast.18, s32[1,128]{1,0:T(1,128)S(1)} %subtract_bitcast_fusion.port_ref, s32[2,8192]{1,0:T(2,128)S(1)} %copy-done.3, s32[2,8192]{1,0:T(2,128)S(1)} %copy-done.4, bf16[2048,128]{1,0:T(8,128)(2,1)S(1)} %bitcast.17, ...), custom_call_target="tpu_custom_call" | custom-call | tf_op jit(solution)/shard_map/pallas_call | solution.py:457
  49.9 0.6 %copy.21 = f32[1,2,32,128]{3,1,2,0:T(2,128)} copy(f32[1,2,32,128]{3,2,1,0:T(8,128)S(1)} %bitcast.19) | data formatting | bytes 65536
Async XLA Ops:
  4.5 2.2 %copy-start = (bf16[64,16,32,32]{0,3,2,1:T(8,128)(2,1)S(1)}, bf16[64,16,32,32]{0,3,2,1:T(8,128)(2,1)}, u32[]{:S(2)}) copy-start(bf16[64,16,32,32]{0,3,2,1:T(8,128)(2,1)} %param.21) | copy-start | bytes 6291460
  6.7 1.0 %copy-start.1 = (bf16[64,32,128]{2,1,0:T(8,128)(2,1)S(1)}, bf16[64,32,128]{2,1,0:T(8,128)(2,1)}, u32[]{:S(2)}) copy-start(bf16[64,32,128]{2,1,0:T(8,128)(2,1)} %param.20) | copy-start | bytes 1572868
  7.8 1.0 %copy-start.2 = (bf16[64,32,128]{2,1,0:T(8,128)(2,1)S(1)}, bf16[64,32,128]{2,1,0:T(8,128)(2,1)}, u32[]{:S(2)}) copy-start(bf16[64,32,128]{2,1,0:T(8,128)(2,1)} %basis_out_ref.1) | copy-start | bytes 1572868
  8.8 0.8 %copy-start.3 = (s32[2,8192]{1,0:T(2,128)S(1)}, s32[2,8192]{1,0:T(2,128)}, u32[]{:S(2)}) copy-start(s32[2,8192]{1,0:T(2,128)} %entry_ref.1) | copy-start | bytes 196612
  9.7 0.8 %copy-start.4 = (s32[2,8192]{1,0:T(2,128)S(1)}, s32[2,8192]{1,0:T(2,128)}, u32[]{:S(2)}) copy-start(s32[2,8192]{1,0:T(2,128)} %sign_ref.1) | copy-start | bytes 196612
  10.5 0.8 %copy-start.5 = (f32[8192]{0:T(1024)S(1)}, f32[8192]{0:T(1024)}, u32[]{:S(2)}) copy-start(f32[8192]{0:T(1024)} %param.17) | copy-start | bytes 98308

commit v5 on v4

--- a/solution.py
+++ b/solution.py
@@ -223,15 +223,18 @@
         index = admissible_ref[:, start : start + 512]
         low = index & (tile_dev - 1)
         owner = index // tile_dev
+        lane = lax.broadcasted_iota(jnp.int32, (1, 512), 1)
+        place = low + (lane & tile_dev)
         tile = lax.broadcasted_iota(jnp.int32, (2 * tile_dev, 512), 0)
-        for c in range(2):
-            hot = jnp.where(tile == low + c * tile_dev, 1.0, 0.0).astype(jnp.bfloat16)
-            found = jnp.dot(held, hot, preferred_element_type=jnp.float32)
-            total = jnp.zeros((rank, 512), jnp.float32)
-            for p in range(peers):
-                total += jnp.where(owner == p, found[p * rank : (p + 1) * rank], 0.0)
-            for j in range(512 // LANES):
-                picked_ref[c, start // LANES + j] = total[:, j * LANES : (j + 1) * LANES]
+        hot = jnp.where(tile == place, 1.0, 0.0).astype(jnp.bfloat16)
+        found = jnp.dot(held, hot, preferred_element_type=jnp.float32)
+        total = jnp.zeros((rank, 512), jnp.float32)
+        for p in range(peers):
+            total += jnp.where(owner == p, found[p * rank : (p + 1) * rank], 0.0)
+        for j in range(512 // LANES):
+            for c in range(2):
+                half = j * LANES + c * tile_dev
+                picked_ref[c, start // LANES + j, :, :tile_dev] = total[:, half : half + tile_dev]
     mixed_ref[...] = jnp.zeros_like(mixed_ref)
 
     @pl.loop(0, rank)
@@ -398,7 +401,6 @@
         mixed_ref,
         voltage_ref,
     )
-    slots_ref[...] = jnp.zeros_like(slots_ref)
     for p in range(peers):
         for c in range(2):
             row = c * rows + mesh_rows + p
@@ -452,7 +454,7 @@
     far_count = admissible.shape[1]
     vmem, hbm = pl.BlockSpec(memory_space=pltpu.VMEM), pl.BlockSpec(memory_space=pl.ANY)
     mixing = coupling.transpose(1, 2, 3, 0)
-    message = pltpu.VMEM((peers, 8, LANES), jnp.float32)
+    message = pltpu.VMEM((peers, 2, LANES), jnp.float32)
     tiles = pltpu.VMEM((2, tile_dev, LANES), jnp.float32)
     made = pl.pallas_call(
         functools.partial(whole_kernel, peers, rows, mesh_rows),
@@ -460,9 +462,9 @@
         in_specs=[vmem] * 7 + [hbm, vmem, hbm] + [vmem] * 3,
         out_specs=vmem,
         scratch_shapes=[
-            pltpu.VMEM((peers, 8, LANES), jnp.int32),
-            message,
-            message,
+            pltpu.VMEM((peers, 1, LANES), jnp.int32),
+            pltpu.VMEM((peers, 4, LANES), jnp.float32),
+            pltpu.VMEM((peers, 4, LANES), jnp.float32),
             tiles,
             pltpu.VMEM((rank, 2 * tile_dev), jnp.bfloat16),
             pltpu.VMEM((peers, rank, 2 * tile_dev), jnp.bfloat16),
@@ -485,7 +487,7 @@
             collective_id=0, has_side_effects=True, vmem_limit_bytes=VMEM_LIMIT
         ),
     )(
-        jnp.pad(need_slots[:, None, :], ((0, 0), (0, 7), (0, 0))),
+        need_slots[:, None, :],
         current,
         port_position,
         branch_entry,
@@ -493,7 +495,7 @@
         basis_in.reshape(tile_dev * rank, tile_width),
         near_source.reshape(-1, 1),
         near_blocks,
-        jnp.pad(admissible.T, ((0, 0), (0, LANES - tile_dev))).reshape(1, -1),
+        jnp.concatenate([admissible.T, admissible.T], axis=1).reshape(1, -1),
         mixing,
         basis_out,
         resistance.reshape(tile_dev, tile_width),

time: 51.2 us -> 50.3 us (0.982)
  Pallas kernels: 38.7 us -> 37.6 us
  other arithmetic: 0.66 us -> 1.5 us
  local copies, waits for them, and re-layouts: 11.2 us -> 10.5 us
    pad x2 -> x0, local copies, waits for them, and re-layouts: 1.4 us -> none  [the longest x1 0.7 us: per_device(): jnp.pad(need_slots[:, None, :], ((0, 0), (0, 7), (0, 0)))]
    pallas_call x1, Pallas kernels: 38.7 us -> 37.6 us  [per_device(): pl.pallas_call(functools.partial(whole_kernel, peers, rows, mesh_rows), o...]
    concatenate x0 -> x1, other arithmetic: none -> 0.85 us  [per_device(): jnp.concatenate([admissible.T, admissible.T], axis=1).reshape(1, -1)]
    unnamed x15 -> x17, local copies, waits for them, and re-layouts: 8.87 us -> 9.57 us
where the time goes in v5:
time: 50.3 us; the launch traced here: 49.7 us
  Pallas kernels  37.6 us (75%)
  local copies, waits for them, and re-layouts  10.5 us (21%)
  other arithmetic  1.5 us (3%)
    pallas_call x1, Pallas kernels, per_device(): pl.pallas_call(functools.partial(whole_kernel, peers, rows, mesh_rows), o...  37.6 us
    unnamed x17, local copies, waits for them, and re-layouts  9.57 us

profile of v5, /device:TPU:0, one launch (start us, length us, event | category | flops | bytes accessed | tf_op | source)
XLA Modules:
  0.0 49.7 jit_solution(979930710546400120)
XLA Ops:
  0.0 0.7 %subtract_bitcast_fusion.port_ref = s32[1,128]{1,0:T(1,128)S(1)} fusion(s32[64]{0:T(128)} %param.24, s32[]{:T(128)S(6)} %mul.3), kind=kLoop, calls=%fused_computation.3 | loop fusion | flops 128 | bytes 772 | tf_op jit(solution)/shard_map/sub | solution.py:451
  0.7 0.8 %pad_add_fusion = s32[16,128]{1,0:T(8,128)S(1)} fusion(s32[16,64]{1,0:T(8,128)} %bitcast.24), kind=kLoop, calls=%fused_computation.2 | loop fusion | flops 2048 | bytes 12288 | tf_op jit(solution)/shard_map/concatenate | solution.py:498
  1.5 0.8 %copy.22 = f32[1,2,32,128]{3,2,1,0:T(8,128)S(1)} copy(f32[1,2,32,128]{3,1,2,0:T(2,128)} %bitcast.23) | data formatting | bytes 65536
  2.3 0.8 %copy.15 = s32[64,4]{1,0:T(8,128)S(1)} copy(s32[64,4]{0,1:T(4,128)} %param.19) | data formatting | bytes 2048 | tf_op args[6]
  3.0 0.1 reshape.25.source_ref
  3.1 0.9 %pad.9.z_ref = f32[2,128,128]{2,1,0:T(8,128)S(1)} pad(f32[2,64,64]{2,1,0:T(8,128)} %param.25, f32[]{:T(128)} %constant.10.clone.1), padding=0_0x0_64x0_64 | pad | bytes 163844 | tf_op jit(solution)/shard_map/jit(_pad)/pad | solution.py:452
  4.0 0.0 copy-start
  4.0 2.2 %copy-done = bf16[64,16,32,32]{0,3,2,1:T(8,128)(2,1)S(1)} copy-done((bf16[64,16,32,32]{0,3,2,1:T(8,128)(2,1)S(1)}, bf16[64,16,32,32]{0,3,2,1:T(8,128)(2,1)}, u32[]{:S(2)}) %copy-start) | copy-done | bytes 2097176
  6.2 0.0 copy-start.1
  6.2 1.0 %copy-done.1 = bf16[64,32,128]{2,1,0:T(8,128)(2,1)S(1)} copy-done((bf16[64,32,128]{2,1,0:T(8,128)(2,1)S(1)}, bf16[64,32,128]{2,1,0:T(8,128)(2,1)}, u32[]{:S(2)}) %copy-start.1) | copy-done | bytes 524312
  7.2 0.0 copy-start.2
  7.2 1.0 %copy-done.2 = bf16[64,32,128]{2,1,0:T(8,128)(2,1)S(1)} copy-done((bf16[64,32,128]{2,1,0:T(8,128)(2,1)S(1)}, bf16[64,32,128]{2,1,0:T(8,128)(2,1)}, u32[]{:S(2)}) %copy-start.2) | copy-done | bytes 524312
  8.3 0.0 copy-start.3
  8.3 0.8 %copy-done.3 = s32[2,8192]{1,0:T(2,128)S(1)} copy-done((s32[2,8192]{1,0:T(2,128)S(1)}, s32[2,8192]{1,0:T(2,128)}, u32[]{:S(2)}) %copy-start.3) | copy-done | bytes 65560
  9.1 0.0 copy-start.4
  9.1 0.8 %copy-done.4 = s32[2,8192]{1,0:T(2,128)S(1)} copy-done((s32[2,8192]{1,0:T(2,128)S(1)}, s32[2,8192]{1,0:T(2,128)}, u32[]{:S(2)}) %copy-start.4) | copy-done | bytes 65560
  9.9 0.0 copy-start.5
  9.9 0.8 %copy-done.5 = f32[8192]{0:T(1024)S(1)} copy-done((f32[8192]{0:T(1024)S(1)}, f32[8192]{0:T(1024)}, u32[]{:S(2)}) %copy-start.5) | copy-done | bytes 32792
  10.7 0.0 copy-start.6
  10.7 0.7 %copy-done.6 = s32[16,128]{1,0:T(8,128)S(1)} copy-done((s32[16,128]{1,0:T(8,128)S(1)}, s32[16,128]{1,0:T(8,128)}, u32[]{:S(2)}) %copy-start.6) | copy-done | bytes 8216
  11.4 37.6 %shard_map.127 = f32[2,32,128]{2,1,0:T(8,128)S(1)} custom-call(s32[16,1,128]{2,1,0:T(1,128)S(1)} %bitcast.22, f32[2,32,128]{2,1,0:T(8,128)S(1)} %bitcast.18, s32[1,128]{1,0:T(1,128)S(1)} %subtract_bitcast_fusion.port_ref, s32[2,8192]{1,0:T(2,128)S(1)} %copy-done.3, s32[2,8192]{1,0:T(2,128)S(1)} %copy-done.4, bf16[2048,128]{1,0:T(8,128)(2,1)S(1)} %bitcast.17, ...), custom_call_target="tpu_custom_call" | custom-call | tf_op jit(solution)/shard_map/pallas_call | solution.py:459
  49.0 0.6 %copy.21 = f32[1,2,32,128]{3,1,2,0:T(2,128)} copy(f32[1,2,32,128]{3,2,1,0:T(8,128)S(1)} %bitcast.19) | data formatting | bytes 65536
Async XLA Ops:
  4.0 2.2 %copy-start = (bf16[64,16,32,32]{0,3,2,1:T(8,128)(2,1)S(1)}, bf16[64,16,32,32]{0,3,2,1:T(8,128)(2,1)}, u32[]{:S(2)}) copy-start(bf16[64,16,32,32]{0,3,2,1:T(8,128)(2,1)} %param.21) | copy-start | bytes 6291460
  6.2 1.0 %copy-start.1 = (bf16[64,32,128]{2,1,0:T(8,128)(2,1)S(1)}, bf16[64,32,128]{2,1,0:T(8,128)(2,1)}, u32[]{:S(2)}) copy-start(bf16[64,32,128]{2,1,0:T(8,128)(2,1)} %param.20) | copy-start | bytes 1572868
  7.2 1.0 %copy-start.2 = (bf16[64,32,128]{2,1,0:T(8,128)(2,1)S(1)}, bf16[64,32,128]{2,1,0:T(8,128)(2,1)}, u32[]{:S(2)}) copy-start(bf16[64,32,128]{2,1,0:T(8,128)(2,1)} %basis_out_ref.1) | copy-start | bytes 1572868
  8.3 0.8 %copy-start.3 = (s32[2,8192]{1,0:T(2,128)S(1)}, s32[2,8192]{1,0:T(2,128)}, u32[]{:S(2)}) copy-start(s32[2,8192]{1,0:T(2,128)} %entry_ref.1) | copy-start | bytes 196612
  9.1 0.8 %copy-start.4 = (s32[2,8192]{1,0:T(2,128)S(1)}, s32[2,8192]{1,0:T(2,128)}, u32[]{:S(2)}) copy-start(s32[2,8192]{1,0:T(2,128)} %sign_ref.1) | copy-start | bytes 196612
  9.9 0.8 %copy-start.5 = (f32[8192]{0:T(1024)S(1)}, f32[8192]{0:T(1024)}, u32[]{:S(2)}) copy-start(f32[8192]{0:T(1024)} %param.17) | copy-start | bytes 98308
  10.7 0.7 %copy-start.6 = (s32[16,128]{1,0:T(8,128)S(1)}, s32[16,128]{1,0:T(8,128)}, u32[]{:S(2)}) copy-start(s32[16,128]{1,0:T(8,128)} %param.16) | copy-start | bytes 24580
